TPU v7x, 512 devices: a whole 4x4x16 slice. The times are simulated.
512 devices in a mesh: loop: 64 (over z, x_lo, core), group: 8 (over y, x_hi).
Axes of the slice: x: 4 (x_hi: 2, x_lo: 2; x = x_hi * 2 + x_lo), y: 4, z: 16, core: 2. Of those that a mesh axis runs over, the one named last changes fastest.
Arguments:
- images: bfloat16 [65536, 1152], P(('loop', 'group')), may hold values from -0.1796875 to 0.1796875
- texts: bfloat16 [65536, 1152], P(('loop', 'group')), may hold values from -0.1796875 to 0.1796875
- image_ids: int32 [65536], P(('loop', 'group')), may hold values from 0 to 511
- text_ids: int32 [65536], P(('loop', 'group')), may hold values from 0 to 511
- logit_scale: float32 [1], replicated, may hold values from 2 to 10
- logit_bias: float32 [1], replicated, may hold values from -4 to -1
Outputs:
- image_grad: float32 [65536, 1152], P(('loop', 'group'))
- text_grad: float32 [65536, 1152], P(('loop', 'group'))
All inputs are finite; a program needn't handle non-finite values.
Results may differ from a plain program's by a relative error of at most 0.0042.
Values may be sent and summed in bfloat16 or wider, within the bound.
A program may use at most 64 MiB of HBM per device.

v0:
```python
import jax
import jax.numpy as jnp
from jax import lax
from jax.sharding import PartitionSpec as P

STEPS = 2


epsilon = 1e-06


def from_behind(value, axis, steps):
    count = lax.axis_size(axis)
    pairs = [(source, (source + steps) % count) for source in range(count)]
    return lax.ppermute(value, axis, pairs)


def unit_rows(rows):
    values = rows.astype(jnp.float32)
    factor = 1.0 / jnp.sqrt(jnp.sum(values * values, axis=-1, keepdims=True) + epsilon)
    return (values * factor, factor)


def pair_terms(image_block, image_keys, text_block, text_keys, scale_value, bias_value):
    logits = (
        scale_value
        * lax.dot_general(
            image_block, text_block, (((1,), (1,)), ((), ())), preferred_element_type=jnp.float32
        )
        + bias_value
    )
    labels = jnp.where(image_keys[:, None] == text_keys[None, :], 1.0, -1.0).astype(jnp.float32)
    weights = (-labels * jax.nn.sigmoid(-labels * logits)).astype(jnp.bfloat16)
    image_part = scale_value * jnp.dot(weights, text_block, preferred_element_type=jnp.float32)
    text_part = scale_value * lax.dot_general(
        weights, image_block, (((0,), (0,)), ((), ())), preferred_element_type=jnp.float32
    )
    return (image_part, text_part)


def unit_backward(grad_unit, direction, factor):
    along = jnp.sum(direction * grad_unit, axis=-1, keepdims=True)
    return factor * (grad_unit - direction * along)


def shards(images, texts, image_ids, text_ids, logit_scale, logit_bias):
    scale_value = logit_scale[0]
    bias_value = logit_bias[0]
    image_dir, image_factor = unit_rows(images)
    text_dir, text_factor = unit_rows(texts)
    image_unit = image_dir.astype(jnp.bfloat16)
    text_unit = text_dir.astype(jnp.bfloat16)
    block_texts, block_keys = (
        lax.all_gather(text_unit, "group", axis=0, tiled=True),
        lax.all_gather(text_ids, "group", axis=0, tiled=True),
    )
    moving_texts, moving_keys = (block_texts, block_keys)
    image_total = jnp.zeros(image_unit.shape, jnp.float32)
    partials = []
    for offset in range(STEPS + 1):
        if offset > 0:
            moving_texts, moving_keys = from_behind((moving_texts, moving_keys), "loop", 1)
        image_part, text_part = pair_terms(
            image_unit, image_ids, moving_texts, moving_keys, scale_value, bias_value
        )
        image_total = image_total + image_part
        partials.append(text_part)
    carried_sum = partials[STEPS]
    for offset in range(STEPS - 1, -1, -1):
        carried_sum = from_behind(carried_sum, "loop", -1) + partials[offset]
    own_text_total = lax.psum_scatter(carried_sum, "group", scatter_dimension=0, tiled=True)
    image_grad = unit_backward(image_total, image_dir, image_factor)
    text_grad = unit_backward(own_text_total, text_dir, text_factor)
    return (image_grad, text_grad)


def solution(mesh):
    in_specs = (
        P(("loop", "group"), None),
        P(("loop", "group"), None),
        P(("loop", "group")),
        P(("loop", "group")),
        P(),
        P(),
    )
    out_specs = (P(("loop", "group"), None), P(("loop", "group"), None))
    return jax.shard_map(shards, mesh=mesh, in_specs=in_specs, out_specs=out_specs, check_vma=False)
```

profile of v0, /device:TPU:1, one launch (start us, length us, event | category | flops | bytes accessed | tf_op | source)
XLA Modules:
  0.0 398.4 jit_solution(1268503722627776817)
XLA Ops:
  7.2 0.0 all-gather.3.cloned.1.call-start
  7.2 1.1 fusion.39
  8.3 1.8 fusion.28
  10.1 0.0 reduce-scatter.2.cloned.1.call-start
  10.2 77.9 %all-gather.3.cloned.1.call-done = bf16[1024,1152]{1,0:T(8,128)(2,1)} async-done(((bf16[128,1152]{1,0:T(8,128)(2,1)}), bf16[1024,1152]{1,0:T(8,128)(2,1)}) %all-gather.3.cloned.1.call-update) | async-done | bytes 2359312 | tf_op jit(solution)/shard_map/all_gather | solution.py:54
  88.0 3.2 collective-permute-start.1
  91.2 26.1 %collective-permute-done.1 = bf16[1024,1152]{1,0:T(8,128)(2,1)S(1)} collective-permute-done((bf16[1024,1152]{1,0:T(8,128)(2,1)}, bf16[1024,1152]{1,0:T(8,128)(2,1)S(1)}, u32[]{:S(2)}, u32[]{:S(2)}) %collective-permute-start.1) | collective-permute-done | bytes 2359328 | tf_op jit(solution)/shard_map/ppermute | solution.py:15
  117.3 4.3 %collective-permute-start.3 = (bf16[1024,1152]{1,0:T(8,128)(2,1)S(1)}, bf16[1024,1152]{1,0:T(8,128)(2,1)S(1)}, u32[]{:S(2)}, u32[]{:S(2)}) collective-permute-start(bf16[1024,1152]{1,0:T(8,128)(2,1)S(1)} %collective-permute-done.1), channel_id=1, source_target_pairs={{0,8},{8,16},{16,24},{24,32},{32,40},{40,48},{48,56},{56,64},{64,7... | collective-permute-start | bytes 7077896 | tf_op jit(solution)/shard_map/ppermute | solution.py:15
  121.6 39.2 %all-gather = s32[8,1,128]{2,1,0:T(1,128)S(1)} all-gather(s32[1,1,128]{2,1,0:T(1,128)} %bitcast.28), channel_id=1, replica_groups=mesh['loop'=64,'group'=8] {'group'}, dimensions={0}, use_global_device_ids=true | all-gather | bytes 4608 | tf_op jit(solution)/shard_map/all_gather | solution.py:55
  160.7 1.9 collective-permute-start
  162.7 1.1 fusion.35
  163.8 3.8 collective-permute-start.2
  168.9 2.2 fusion.25
  171.2 0.9 convolution_multiply_fusion.2
  172.1 4.2 %collective-permute-start.4 = (f32[1024,1152]{1,0:T(8,128)S(1)}, f32[1024,1152]{1,0:T(8,128)S(1)}, u32[]{:S(2)}, u32[]{:S(2)}) collective-permute-start(f32[1024,1152]{1,0:T(8,128)S(1)} %convolution_multiply_fusion.2), channel_id=1, source_target_pairs={{0,504},{8,0},{16,8},{24,16},{32,24},{40,32},{48,40},{56,48},{64,5... | collective-permute-start | bytes 14155784 | tf_op jit(solution)/shard_map/ppermute | solution.py:15
  176.4 1.0 fusion.24
  177.3 50.2 %collective-permute-done.4 = f32[1024,1152]{1,0:T(8,128)S(1)} collective-permute-done((f32[1024,1152]{1,0:T(8,128)S(1)}, f32[1024,1152]{1,0:T(8,128)S(1)}, u32[]{:S(2)}, u32[]{:S(2)}) %collective-permute-start.4) | collective-permute-done | bytes 4718624 | tf_op jit(solution)/shard_map/ppermute | solution.py:15
  227.5 0.9 fusion
  228.4 3.2 collective-permute-start.5
  231.6 1.0 fusion.23
  232.6 0.9 convolution_multiply_fusion
  233.5 50.3 %collective-permute-done.5 = f32[1024,1152]{1,0:T(8,128)S(1)} collective-permute-done((f32[1024,1152]{1,0:T(8,128)S(1)}, f32[1024,1152]{1,0:T(8,128)S(1)}, u32[]{:S(2)}, u32[]{:S(2)}) %collective-permute-start.5) | collective-permute-done | bytes 4718624 | tf_op jit(solution)/shard_map/ppermute | solution.py:15
  283.8 2.6 add.65
  286.5 0.5 fusion.46
  287.0 1.1 copy-done.6
  288.1 0.5 convolution_add_fusion.1
  288.6 1.1 copy-done.4
  289.8 0.6 fusion.32
  290.4 1.0 fusion.34
  291.4 96.8 %reduce-scatter.2.cloned.1.call-done = f32[128,1152]{1,0:T(8,128)} async-done(((f32[1024,1152]{1,0:T(8,128)}), f32[128,1152]{1,0:T(8,128)}) %reduce-scatter.2.cloned.1.call-update) | async-done | bytes 589840 | tf_op jit(solution)/shard_map/reduce_scatter | solution.py:71
  388.2 1.3 fusion.36
  389.5 2.1 fusion.38
  (21 shorter events, 0.1 us)
Async XLA Ops:
  7.2 80.9 %all-gather.3.cloned.1.call-start = ((), (), s32[]{:S(2)}) async-start(), calls=%async_computation.1 | async-start | bytes 2654208 | tf_op jit(solution)/shard_map/all_gather | solution.py:54
  10.1 378.1 %reduce-scatter.2.cloned.1.call-start = ((), (), s32[]{:S(2)}) async-start(), calls=%async_computation.2 | async-start | bytes 5308416 | tf_op jit(solution)/shard_map/reduce_scatter | solution.py:71
  88.0 29.2 %collective-permute-start.1 = (bf16[1024,1152]{1,0:T(8,128)(2,1)}, bf16[1024,1152]{1,0:T(8,128)(2,1)S(1)}, u32[]{:S(2)}, u32[]{:S(2)}) collective-permute-start(bf16[1024,1152]{1,0:T(8,128)(2,1)} %all-gather.3.cloned.1.call-done), channel_id=1, source_target_pairs={{0,8},{8,16},{16,24},{24,32},{32,40},{40,48},{48,56},{56,64},{64,7... | collective-permute-start | bytes 7077896 | tf_op jit(solution)/shard_map/ppermute | solution.py:15
  117.3 59.0 %copy-start.5 = (bf16[1024,1152]{1,0:T(8,128)(2,1)}, bf16[1024,1152]{1,0:T(8,128)(2,1)S(1)}, u32[]{:S(2)}) copy-start(bf16[1024,1152]{1,0:T(8,128)(2,1)S(1)} %collective-permute-done.1) | copy-start | bytes 7077892
  117.3 51.6 %collective-permute-start.3 = (bf16[1024,1152]{1,0:T(8,128)(2,1)S(1)}, bf16[1024,1152]{1,0:T(8,128)(2,1)S(1)}, u32[]{:S(2)}, u32[]{:S(2)}) collective-permute-start(bf16[1024,1152]{1,0:T(8,128)(2,1)S(1)} %collective-permute-done.1), channel_id=1, source_target_pairs={{0,8},{8,16},{16,24},{24,32},{32,40},{40,48},{48,56},{56,64},{64,7... | collective-permute-start | bytes 7077896 | tf_op jit(solution)/shard_map/ppermute | solution.py:15
  160.7 3.0 collective-permute-start
  163.8 5.1 %collective-permute-start.2 = (s32[1024]{0:T(1024)S(1)}, s32[1024]{0:T(1024)S(1)}, u32[]{:S(2)}, u32[]{:S(2)}) collective-permute-start(s32[1024]{0:T(1024)S(1)} %collective-permute-done), channel_id=1, source_target_pairs={{0,8},{8,16},{16,24},{24,32},{32,40},{40,48},{48,56},{56,64},{64,7... | collective-permute-start | bytes 12296 | tf_op jit(solution)/shard_map/ppermute | solution.py:15
  168.9 2.3 copy-start.3
  168.9 2.3 copy-start
  171.2 5.1 %copy-start.7 = (s32[128]{0:T(128)S(1)}, s32[128]{0:T(128)}, u32[]{:S(2)}) copy-start(s32[128]{0:T(128)} %param.8) | copy-start | bytes 1540
  172.1 55.4 %collective-permute-start.4 = (f32[1024,1152]{1,0:T(8,128)S(1)}, f32[1024,1152]{1,0:T(8,128)S(1)}, u32[]{:S(2)}, u32[]{:S(2)}) collective-permute-start(f32[1024,1152]{1,0:T(8,128)S(1)} %convolution_multiply_fusion.2), channel_id=1, source_target_pairs={{0,504},{8,0},{16,8},{24,16},{32,24},{40,32},{48,40},{56,48},{64,5... | collective-permute-start | bytes 14155784 | tf_op jit(solution)/shard_map/ppermute | solution.py:15
  227.5 4.1 %copy-start.2 = (bf16[1024,1152]{1,0:T(8,128)(2,1)S(1)}, bf16[1024,1152]{1,0:T(8,128)(2,1)}, u32[]{:S(2)}) copy-start(bf16[1024,1152]{1,0:T(8,128)(2,1)} %all-gather.3.cloned.1.call-done) | copy-start | bytes 7077892
  228.4 55.4 %collective-permute-start.5 = (f32[1024,1152]{1,0:T(8,128)S(1)}, f32[1024,1152]{1,0:T(8,128)S(1)}, u32[]{:S(2)}, u32[]{:S(2)}) collective-permute-start(f32[1024,1152]{1,0:T(8,128)S(1)} %fusion), channel_id=1, source_target_pairs={{0,504},{8,0},{16,8},{24,16},{32,24},{40,32},{48,40},{56,48},{64,5... | collective-permute-start | bytes 14155784 | tf_op jit(solution)/shard_map/ppermute | solution.py:15
  286.4 1.7 copy-start.6
  288.1 1.7 copy-start.4
  289.8 98.4 %copy-start.1 = (bf16[128,1152]{1,0:T(8,128)(2,1)S(1)}, bf16[128,1152]{1,0:T(8,128)(2,1)}, u32[]{:S(2)}) copy-start(bf16[128,1152]{1,0:T(8,128)(2,1)} %param.7) | copy-start | bytes 884740
Sparse Core Ops, SparseCore 0:
  11.7 76.2 all-gather.2
  286.6 101.5 reduce-scatter.1
where the time goes:
time: 399 us; the launch traced here: 398 us
  waiting for transfers between devices  301 us (75%)
  blocking collectives  39.2 us (10%)
  starting transfers between devices  20.7 us (5%)
  between operations  15.5 us (4%)
  other arithmetic  11 us (3%)
  matrix products  8.4 us (2%)
    ppermute x6, waiting for transfers between devices, from_behind(): return lax.ppermute(value, axis, pairs)  127 us
    reduce_scatter x1, waiting for transfers between devices, shards(): lax.psum_scatter(carried_sum, 'group', scatter_dimension=0, tiled=True)  96.8 us
    all_gather x1, waiting for transfers between devices, shards(): lax.all_gather(text_unit, 'group', axis=0, tiled=True)  77.9 us
    all_gather x1, blocking collectives, shards(): lax.all_gather(text_ids, 'group', axis=0, tiled=True)  39.2 us
    ppermute x6, starting transfers between devices, from_behind(): return lax.ppermute(value, axis, pairs)  20.6 us
  transfers between devices with their start and end apart: 8, of which 5 were waited for; matrix products, arithmetic and copies ran while one was open for 2% of the time, Pallas kernels for 0%

commit v1 on v0

v1 whole, which is shorter than its diff:
```python
import functools

import jax
import jax.numpy as jnp
from jax import lax
from jax.experimental import pallas as pl
from jax.experimental.pallas import tpu as pltpu
from jax.sharding import PartitionSpec as P

epsilon = 1e-06
CHUNKS = 3
MESH = pl.DeviceIdType.MESH
F32, BF16 = jnp.float32, jnp.bfloat16


def kernel(
    n_loop, images, texts, image_ids, text_ids, scale, bias, image_out, text_out,
    img, txt, idi, idt, w, wt, gt, gi, oc_s, oc_r, z_s, z_r, d_s, d_r, x_s, x_r, h_s, h_r, y_s, y_r,
    gx_s, gx_r, gf_s, gf_r, gz_s, gz_r, go_s, go_r, gy_s, gy_r, gh_s, gh_r, id_s, id_r,
    ro_s, ro_r, rz_s, rz_r, rd_s, rd_r, rx_s, rx_r, rh_s, rh_r, ry_s, ry_r,
):
    R = images.shape[0]
    H = R // 2
    D = images.shape[1]
    C = CHUNKS
    DC = D // C
    loop, group = lax.axis_index("loop"), lax.axis_index("group")
    core = lax.rem(loop, 2)
    x_lo = lax.rem(loop // 2, 2)
    y, x_hi = group // 2, lax.rem(group, 2)
    flip = loop + 2 - 4 * x_lo
    other = (loop + 1 - 2 * core, group)
    near_a = (flip, group)
    near_b = (flip, group + 1 - 2 * x_hi)
    y_up = (loop, lax.rem(y + 1, 4) * 2 + x_hi)
    y_down = (loop, lax.rem(y + 3, 4) * 2 + x_hi)
    z_up = (lax.rem(loop + 4, n_loop), group)
    z_down = (lax.rem(loop + n_loop - 4, n_loop), group)
    x_near = (near_a, near_b)
    y_near = (y_up, y_down)
    low = x_lo == 0
    mine = 6 - 2 * x_lo
    theirs = 4 + 2 * x_lo

    barrier = pltpu.get_barrier_semaphore()
    for device in (other, near_a, near_b, y_up, y_down):
        pl.semaphore_signal(barrier, inc=1, device_id=device, device_id_type=MESH)

    @pl.when(low)
    def _():
        for device in (z_up, z_down):
            pl.semaphore_signal(barrier, inc=1, device_id=device, device_id_type=MESH)

    def normalize(rows, block):
        values = rows[...].astype(F32)
        factor = 1.0 / jnp.sqrt(jnp.sum(values * values, axis=-1, keepdims=True) + epsilon)
        for ch in range(C):
            block[ch, 0:R, :] = (values[:, ch * DC:(ch + 1) * DC] * factor).astype(BF16)

    normalize(texts, txt)
    idt[0] = text_ids[...]
    idi[0] = image_ids[...]
    pl.semaphore_wait(barrier, 7 - 2 * x_lo)

    def rows_of(slot, count=1):
        return pl.ds(pl.multiple_of(slot * R, R), count * R)

    def send(src, dst, s, r, device):
        return pltpu.make_async_remote_copy(
            src_ref=src, dst_ref=dst, send_sem=s, recv_sem=r, device_id=device, device_id_type=MESH)

    def gx(ch, i):
        return send(txt.at[ch, 0:R], txt.at[ch, rows_of(theirs + i)], gx_s.at[i, ch], gx_r.at[i, ch], x_near[i])

    def gf(ch, i):
        return send(txt.at[ch, pl.ds(pl.multiple_of((mine + i) * R + i * H, H), H)],
                    txt.at[ch, R + i * H:R + (i + 1) * H], gf_s.at[i, ch], gf_r.at[i, ch], x_near[1 - i])

    def gz(ch, i):
        return send(txt.at[ch, (6 + i) * R:(7 + i) * R], txt.at[ch, (4 + i) * R:(5 + i) * R],
                    gz_s.at[i, ch], gz_r.at[i, ch], z_up)

    def go(ch, i):
        return send(txt.at[ch, rows_of(4 * core + i)], txt.at[ch, (2 + i) * R:(3 + i) * R],
                    go_s.at[i, ch], go_r.at[i, ch], other)

    def gy(ch, i):
        return send(img.at[ch, 0:R], img.at[ch, (1 + i) * R:(2 + i) * R], gy_s.at[i, ch], gy_r.at[i, ch], y_near[i])

    def gh(ch, i):
        return send(img.at[ch, (1 + i) * R + i * H:(1 + i) * R + (i + 1) * H],
                    img.at[ch, 3 * R + i * H:3 * R + (i + 1) * H], gh_s.at[i, ch], gh_r.at[i, ch], y_near[i])

    id_x = [send(idt.at[0], idt.at[theirs + i], id_s.at[i], id_r.at[i], x_near[i]) for i in range(2)]
    id_f = send(idt.at[mine], idt.at[1], id_s.at[2], id_r.at[2], near_b)
    id_z = send(idt.at[6:8], idt.at[4:6], id_s.at[3], id_r.at[3], z_up)
    id_o = send(idt.at[pl.ds(4 * core, 2)], idt.at[2:4], id_s.at[4], id_r.at[4], other)
    id_y = [send(idi.at[0], idi.at[1 + i], id_s.at[5 + i], id_r.at[5 + i], y_near[i]) for i in range(2)]
    id_h = send(idi.at[1], idi.at[3], id_s.at[7], id_r.at[7], y_up)

    for ch in range(C):
        for i in range(2):
            gx(ch, i).start()
    for copy in id_x:
        copy.start()
    normalize(images, img)
    for ch in range(C):
        for i in range(2):
            gy(ch, i).start()
    for copy in id_y:
        copy.start()

    @pl.when(core == 0)
    def _():
        for ch in range(C):
            go(ch, 0).start()

    for ch in range(C):
        for i in range(2):
            gx(ch, i).wait_recv()

            @pl.when(low)
            def _():
                gz(ch, i).start()

            gf(ch, i).start()

            @pl.when((x_lo == 1) & (core == 1))
            def _():
                go(ch, i).start()

        for i in range(2):
            gy(ch, i).wait_recv()
            gh(ch, i).start()
    for copy in id_x:
        copy.wait_recv()
    id_f.start()

    @pl.when(low)
    def _():
        id_z.start()

    for copy in id_y:
        copy.wait_recv()
    id_h.start()
    id_f.wait_recv()

    @pl.when(low)
    def _():
        id_z.wait_recv()

    id_o.start()

    for ch in range(C):
        for i in range(2):
            gf(ch, i).wait_recv()

        @pl.when(core == 0)
        def _():
            go(ch, 1).start()

        @pl.when(low)
        def _():
            for i in range(2):
                gz(ch, i).wait_recv()

        @pl.when(low & (core == 1))
        def _():
            for i in range(2):
                go(ch, i).start()

        for i in range(2):
            gh(ch, i).wait_recv()
    id_h.wait_recv()
    id_o.wait_recv()
    for ch in range(C):
        for i in range(2):
            go(ch, i).wait_recv()

    image_keys = jnp.concatenate(
        [jnp.transpose(jnp.broadcast_to(idi[s], (128, R)))[:, 0:1] for s in range(4)], axis=0)
    scale_value, bias_value = scale[0], bias[0]

    def weigh(j, carry):
        rows = pl.ds(pl.multiple_of(j * 2 * R, 2 * R), 2 * R)
        dots = None
        for ch in range(C):
            part = lax.dot_general(
                img[ch], txt[ch, rows, :], (((1,), (1,)), ((), ())), preferred_element_type=F32)
            dots = part if dots is None else dots + part
        logits = scale_value * dots + bias_value
        text_keys = jnp.concatenate([idt[2 * j], idt[2 * j + 1]], axis=1)
        same = image_keys == text_keys
        share = jax.nn.sigmoid(jnp.where(same, -logits, logits))
        weights = jnp.where(same, -share, share)
        w[j] = weights.astype(BF16)
        wt[j] = jnp.transpose(weights).astype(BF16)
        return carry

    lax.fori_loop(0, 3, weigh, 0)

    def ro(ch):
        return send(oc_s.at[ch], oc_r.at[ch], ro_s.at[ch], ro_r.at[ch], other)

    def rz(ch):
        return send(z_s.at[ch], z_r.at[ch], rz_s.at[ch], rz_r.at[ch], z_down)

    def rd(ch, i):
        return send(d_s.at[ch, i * H:(i + 1) * H], d_r.at[ch, i * H:(i + 1) * H],
                    rd_s.at[i, ch], rd_r.at[i, ch], x_near[i])

    def rx(ch, i):
        return send(x_s.at[ch, i], x_r.at[ch, i], rx_s.at[i, ch], rx_r.at[i, ch], x_near[i])

    def rh(ch, i):
        return send(h_s.at[ch, i * H:(i + 1) * H], h_r.at[ch, i * H:(i + 1) * H],
                    rh_s.at[i, ch], rh_r.at[i, ch], y_near[i])

    def ry(ch, i):
        return send(y_s.at[ch, i], y_r.at[ch, i], ry_s.at[i, ch], ry_r.at[i, ch], y_near[i])

    for ch in range(C):
        def text_part(j, carry, ch=ch):
            rows = pl.ds(pl.multiple_of(j * 2 * R, 2 * R), 2 * R)
            gt[ch, rows, :] = jnp.dot(wt[j], img[ch], preferred_element_type=F32)
            return carry

        lax.fori_loop(0, 3, text_part, 0)
        oc_s[ch] = gt[ch, 2 * R:4 * R, :].astype(BF16)
        ro(ch).start()

        def image_part(i, carry, ch=ch):
            rows = pl.ds(pl.multiple_of(i * 2 * R, 2 * R), 2 * R)
            total = None
            for j in range(3):
                part = jnp.dot(w[j, rows, :], txt[ch, 2 * j * R:2 * (j + 1) * R, :], preferred_element_type=F32)
                total = part if total is None else total + part
            gi[ch, rows, :] = total
            return carry

        lax.fori_loop(0, 2, image_part, 0)
        h_s[ch] = gi[ch, 3 * R:4 * R, :].astype(BF16)
        for i in range(2):
            rh(ch, i).start()

    for ch in range(C):
        ro(ch).wait_recv()
        at = pl.ds(pl.multiple_of(4 * core * R, 2 * R), 2 * R)
        gt[ch, at, :] = gt[ch, at, :] + oc_r[ch].astype(F32)

        @pl.when(low)
        def _():
            z_s[ch] = gt[ch, 4 * R:6 * R, :].astype(BF16)
            rz(ch).start()

        d_s[ch] = gt[ch, R:2 * R, :].astype(BF16)
        for i in range(2):
            rd(ch, i).start()
        for i in range(2):
            rh(ch, i).wait_recv()
        y_s[ch, 0, 0:H] = (gi[ch, 2 * R:2 * R + H, :] + h_r[ch, 0:H].astype(F32)).astype(BF16)
        y_s[ch, 0, H:R] = gi[ch, 2 * R + H:3 * R, :].astype(BF16)
        y_s[ch, 1, 0:H] = gi[ch, R:R + H, :].astype(BF16)
        y_s[ch, 1, H:R] = (gi[ch, R + H:2 * R, :] + h_r[ch, H:R].astype(F32)).astype(BF16)
        for i in range(2):
            ry(ch, i).start()

    for ch in range(C):
        @pl.when(low)
        def _():
            rz(ch).wait_recv()
            gt[ch, 4 * R:6 * R, :] = z_r[ch].astype(F32)

        for i in range(2):
            rd(ch, i).wait_recv()
        x_s[ch, 0, 0:H] = gt[ch, 4 * R:4 * R + H, :].astype(BF16)
        x_s[ch, 0, H:R] = (gt[ch, 4 * R + H:5 * R, :] + d_r[ch, H:R].astype(F32)).astype(BF16)
        x_s[ch, 1, 0:H] = (gt[ch, 5 * R:5 * R + H, :] + d_r[ch, 0:H].astype(F32)).astype(BF16)
        x_s[ch, 1, H:R] = gt[ch, 5 * R + H:6 * R, :].astype(BF16)
        for i in range(2):
            rx(ch, i).start()

    def backward(rows, parts, out):
        values = rows[...].astype(F32)
        factor = 1.0 / jnp.sqrt(jnp.sum(values * values, axis=-1, keepdims=True) + epsilon)
        unit = values * factor
        grad = scale_value * jnp.concatenate(parts, axis=-1)
        along = jnp.sum(unit * grad, axis=-1, keepdims=True)
        out[...] = factor * (grad - unit * along)

    for ch in range(C):
        for i in range(2):
            ry(ch, i).wait_recv()
    backward(images, [gi[ch, 0:R, :] + (y_r[ch, 0].astype(F32) + y_r[ch, 1].astype(F32)) for ch in range(C)],
             image_out)
    for ch in range(C):
        for i in range(2):
            rx(ch, i).wait_recv()
    backward(texts, [gt[ch, 0:R, :] + (x_r[ch, 0].astype(F32) + x_r[ch, 1].astype(F32)) for ch in range(C)],
             text_out)

    for ch in range(C):
        for i in range(2):
            for copy in (gx, gf, go, gy, gh, rd, rx, rh, ry):
                copy(ch, i).wait_send()
        ro(ch).wait_send()
    for copy in id_x + id_y + [id_f, id_o, id_h]:
        copy.wait_send()

    @pl.when(low)
    def _():
        id_z.wait_send()
        for ch in range(C):
            rz(ch).wait_send()
            for i in range(2):
                gz(ch, i).wait_send()


def shards(n_loop, images, texts, image_ids, text_ids, logit_scale, logit_bias):
    R, D = images.shape
    C = CHUNKS
    DC = D // C
    dma = pltpu.SemaphoreType.DMA
    vmem = pl.BlockSpec(memory_space=pltpu.VMEM)
    smem = pl.BlockSpec(memory_space=pltpu.SMEM)
    pair = lambda: [dma((2, C)), dma((2, C))]
    single = lambda: [dma((C,)), dma((C,))]
    return pl.pallas_call(
        functools.partial(kernel, n_loop),
        out_shape=(jax.ShapeDtypeStruct((R, D), F32), jax.ShapeDtypeStruct((R, D), F32)),
        in_specs=[vmem, vmem, vmem, vmem, smem, smem],
        out_specs=(vmem, vmem),
        scratch_shapes=[
            pltpu.VMEM((C, 4 * R, DC), BF16),
            pltpu.VMEM((C, 8 * R, DC), BF16),
            pltpu.VMEM((4, 1, R), jnp.int32),
            pltpu.VMEM((8, 1, R), jnp.int32),
            pltpu.VMEM((3, 4 * R, 2 * R), BF16),
            pltpu.VMEM((3, 2 * R, 4 * R), BF16),
            pltpu.VMEM((C, 6 * R, DC), F32),
            pltpu.VMEM((C, 4 * R, DC), F32),
            pltpu.VMEM((C, 2 * R, DC), BF16),
            pltpu.VMEM((C, 2 * R, DC), BF16),
            pltpu.VMEM((C, 2 * R, DC), BF16),
            pltpu.VMEM((C, 2 * R, DC), BF16),
            pltpu.VMEM((C, R, DC), BF16),
            pltpu.VMEM((C, R, DC), BF16),
            pltpu.VMEM((C, 2, R, DC), BF16),
            pltpu.VMEM((C, 2, R, DC), BF16),
            pltpu.VMEM((C, R, DC), BF16),
            pltpu.VMEM((C, R, DC), BF16),
            pltpu.VMEM((C, 2, R, DC), BF16),
            pltpu.VMEM((C, 2, R, DC), BF16),
        ] + pair() + pair() + pair() + pair() + pair() + pair() + [dma((8,)), dma((8,))]
        + single() + single() + pair() + pair() + pair() + pair(),
        compiler_params=pltpu.CompilerParams(
            collective_id=0, has_side_effects=True, vmem_limit_bytes=48 * 1024 * 1024),
        cost_estimate=pl.CostEstimate(
            flops=6 * 4 * R * 6 * R * D, bytes_accessed=12 * R * D, transcendentals=24 * R * R),
    )(images, texts, image_ids.reshape(1, R), text_ids.reshape(1, R), logit_scale, logit_bias)


def solution(mesh):
    rows = P(("loop", "group"), None)
    ids = P(("loop", "group"))
    return jax.shard_map(
        functools.partial(shards, mesh.shape["loop"]), mesh=mesh,
        in_specs=(rows, rows, ids, ids, P(), P()), out_specs=(rows, rows), check_vma=False)
```

time: 399 us -> 60.8 us (0.15)
  waiting for transfers between devices: 301 us -> 0 us
  Pallas kernels: 0 us -> 53.7 us
  blocking collectives: 39.2 us -> 0 us
  starting transfers between devices: 20.7 us -> 0 us
  between operations: 15.5 us -> 1.95 us
  other arithmetic: 11 us -> 0 us
  matrix products: 8.4 us -> 0 us
    ppermute x6 -> x0, waiting for transfers between devices: 127 us -> none  [from_behind(): return lax.ppermute(value, axis, pairs)]
    reduce_scatter x1 -> x0, waiting for transfers between devices: 96.8 us -> none  [shards(): lax.psum_scatter(carried_sum, 'group', scatter_dimension=0, tiled=True)]
    all_gather x1 -> x0, waiting for transfers between devices: 77.9 us -> none  [shards(): lax.all_gather(text_unit, 'group', axis=0, tiled=True)]
    pallas_call x0 -> x1, Pallas kernels: none -> 53.7 us  [shards(): pl.pallas_call(functools.partial(kernel, n_loop), out_shape=(jax.ShapeDty...]
    all_gather x1 -> x0, blocking collectives: 39.2 us -> none  [shards(): lax.all_gather(text_ids, 'group', axis=0, tiled=True)]
    ppermute x6 -> x0, starting transfers between devices: 20.6 us -> none  [from_behind(): return lax.ppermute(value, axis, pairs)]
    dot_general x9 -> x0, matrix products: 8.4 us -> none  [the longest x3 4.21 us: pair_terms(): lax.dot_general(image_block, text_block, (((1,), (1,)), ((), ())), prefer...]
  transfers between devices with their start and end apart: 8 -> 0, of which waited for: 5 -> 0; matrix products, arithmetic and copies ran while one was open for 2% -> 0% of each run, Pallas kernels for 0% -> 0%
where the time goes in v1:
time: 60.8 us; the launch traced here: 59.8 us
  Pallas kernels  53.7 us (88%)
  local copies, waits for them, and re-layouts  4.21 us (7%)
  between operations  1.95 us (3%)
    pallas_call x1, Pallas kernels, shards(): pl.pallas_call(functools.partial(kernel, n_loop), out_shape=(jax.ShapeDty...  53.7 us
    unnamed x10, local copies, waits for them, and re-layouts  4.21 us

profile of v1, /device:TPU:1, one launch (start us, length us, event | category | flops | bytes accessed | tf_op | source)
XLA Modules:
  0.0 59.8 jit_solution(5862829874386033864)
XLA Ops:
  1.9 0.0 copy-start.2
  1.9 0.0 copy-start.3
  1.9 0.6 %copy-done.2 = s32[128]{0:T(128)S(1)} copy-done((s32[128]{0:T(128)S(1)}, s32[128]{0:T(128)}, u32[]{:S(2)}) %copy-start.2) | copy-done | bytes 536
  2.6 0.0 copy-done.3
  2.6 0.0 copy-start
  2.6 1.0 %copy-done = bf16[128,1152]{1,0:T(8,128)(2,1)S(1)} copy-done((bf16[128,1152]{1,0:T(8,128)(2,1)S(1)}, bf16[128,1152]{1,0:T(8,128)(2,1)}, u32[]{:S(2)}) %copy-start) | copy-done | bytes 294936
  3.6 0.0 copy-start.1
  3.6 1.0 %copy-done.1 = bf16[128,1152]{1,0:T(8,128)(2,1)S(1)} copy-done((bf16[128,1152]{1,0:T(8,128)(2,1)S(1)}, bf16[128,1152]{1,0:T(8,128)(2,1)}, u32[]{:S(2)}) %copy-start.1) | copy-done | bytes 294936
  4.5 53.7 %shard_map.77 = (f32[128,1152]{1,0:T(8,128)S(1)}, f32[128,1152]{1,0:T(8,128)S(1)}) custom-call(bf16[128,1152]{1,0:T(8,128)(2,1)S(1)} %copy-done, bf16[128,1152]{1,0:T(8,128)(2,1)S(1)} %copy-done.1, s32[1,128]{1,0:T(1,128)S(1)} %bitcast.2, s32[1,128]{1,0:T(1,128)S(1)} %bitcast.3, f32[1]{0:T(128)S(6)} %copy.10.scale, f32[1]{0:T(128)S(6)} %copy.11.bias), custom_call_target="tpu_custom_call" | custom-call | flops 2717908992 | bytes 1769472 | tf_op jit(solution)/shard_map/pallas_call | solution.py:328
  58.2 0.8 %copy.12 = f32[128,1152]{1,0:T(8,128)} copy(f32[128,1152]{1,0:T(8,128)S(1)} %get-tuple-element.4) | data formatting | bytes 1179648
  59.0 0.8 %copy.13 = f32[128,1152]{1,0:T(8,128)} copy(f32[128,1152]{1,0:T(8,128)S(1)} %get-tuple-element.5) | data formatting | bytes 1179648
Async XLA Ops:
  1.9 0.7 %copy-start.2 = (s32[128]{0:T(128)S(1)}, s32[128]{0:T(128)}, u32[]{:S(2)}) copy-start(s32[128]{0:T(128)} %param.8) | copy-start | bytes 1540
  1.9 0.7 %copy-start.3 = (s32[128]{0:T(128)S(1)}, s32[128]{0:T(128)}, u32[]{:S(2)}) copy-start(s32[128]{0:T(128)} %param.9) | copy-start | bytes 1540
  2.6 1.0 %copy-start = (bf16[128,1152]{1,0:T(8,128)(2,1)S(1)}, bf16[128,1152]{1,0:T(8,128)(2,1)}, u32[]{:S(2)}) copy-start(bf16[128,1152]{1,0:T(8,128)(2,1)} %images.1) | copy-start | bytes 884740
  3.6 1.0 %copy-start.1 = (bf16[128,1152]{1,0:T(8,128)(2,1)S(1)}, bf16[128,1152]{1,0:T(8,128)(2,1)}, u32[]{:S(2)}) copy-start(bf16[128,1152]{1,0:T(8,128)(2,1)} %texts.1) | copy-start | bytes 884740

commit v2 on v0

v2 whole, which is shorter than its diff:
```python
import functools

import jax
import jax.numpy as jnp
from jax import lax
from jax.experimental import pallas as pl
from jax.experimental.pallas import tpu as pltpu
from jax.sharding import PartitionSpec as P

epsilon = 1e-06
MESH = pl.DeviceIdType.MESH
F32, BF16 = jnp.float32, jnp.bfloat16
TILE = 384


def kernel(
    n_loop, images, texts, image_ids, text_ids, scale, bias, image_out, text_out,
    raw_i, raw_t, img, txt, idi, idt, keys, w, wt, gt, gi,
    oc_s, oc_r, d_s, d_r, c_s, c_r, z_r, x_s, x_r, h_s, h_r, y_s, y_r,
    load, gx_s, gx_r, g2_s, g2_r, gf_s, gf_r, gz_s, gz_r, go_s, go_r, gy_s, gy_r, gw_s, gw_r, gh_s, gh_r, id_s, id_r,
    ro_s, ro_r, rd_s, rd_r, rc_s, rc_r, rz_s, rz_r, rx_s, rx_r, rh_s, rh_r, rn_s, rn_r, ra_s, ra_r,
):
    R, D = raw_i.shape
    H = R // 2
    loop, group = lax.axis_index("loop"), lax.axis_index("group")
    core = lax.rem(loop, 2)
    x_lo = lax.rem(loop // 2, 2)
    y, x_hi = group // 2, lax.rem(group, 2)
    flip = loop + 2 - 4 * x_lo
    other = (loop + 1 - 2 * core, group)
    x_near = ((flip, group), (flip, group + 1 - 2 * x_hi))
    y_near = ((loop, lax.rem(y + 1, 4) * 2 + x_hi), (loop, lax.rem(y + 3, 4) * 2 + x_hi))
    z_up = (lax.rem(loop + 4, n_loop), group)
    z_down = (lax.rem(loop + n_loop - 4, n_loop), group)
    low, high = x_lo == 0, x_lo == 1

    loads = [
        pltpu.make_async_copy(src, dst, load.at[i])
        for i, (src, dst) in enumerate(
            [(texts, raw_t), (images, raw_i), (text_ids, idt.at[0]), (image_ids, idi.at[0])])
    ]
    for copy in loads:
        copy.start()
    barrier = pltpu.get_barrier_semaphore()
    for device in (*x_near, *y_near, z_down, other):
        pl.semaphore_signal(barrier, inc=1, device_id=device, device_id_type=MESH)

    def normalize(rows, block):
        values = rows[...].astype(F32)
        factor = 1.0 / jnp.sqrt(jnp.sum(values * values, axis=-1, keepdims=True) + epsilon)
        block[0:R, :] = (values * factor).astype(BF16)

    def send(src, dst, s, r, device):
        return pltpu.make_async_remote_copy(
            src_ref=src, dst_ref=dst, send_sem=s, recv_sem=r, device_id=device, device_id_type=MESH)

    def half(ref, slot, h):
        at = slot * R + h * H
        return ref.at[pl.ds(at if isinstance(at, int) else pl.multiple_of(at, H), H)]

    def block(ref, slot):
        at = slot * R
        return ref.at[pl.ds(at if isinstance(at, int) else pl.multiple_of(at, R), R)]

    def gx(i):
        return send(half(txt, 0, i), half(txt, 4 + 2 * x_lo + i, i), gx_s.at[i], gx_r.at[i], x_near[i])

    def g2(i):
        return send(half(txt, 6 * x_lo, 1 - i), half(txt, 4 + i, 1 - i), g2_s.at[i], g2_r.at[i], x_near[i])

    def gf(i):
        return send(half(txt, 6 - 2 * x_lo + i, i), half(txt, 1, i), gf_s.at[i], gf_r.at[i], x_near[1 - i])

    def gz(i):
        return send(half(txt, (6 + i) * (1 - x_lo), i), half(txt, 4 + i + x_lo * (2 - i), i),
                    gz_s.at[i], gz_r.at[i], z_up)

    def go(i):
        return send(block(txt, 4 * core + i), block(txt, 2 + i), go_s.at[i], go_r.at[i], other)

    def gy(i):
        return send(half(img, 0, i), half(img, 1 + i, i), gy_s.at[i], gy_r.at[i], y_near[i])

    def gw(i):
        return send(half(img, 0, 1 - i), half(img, 1 + i, 1 - i), gw_s.at[i], gw_r.at[i], y_near[i])

    def gh(i):
        return send(half(img, 1 + i, i), half(img, 3, i), gh_s.at[i], gh_r.at[i], y_near[i])

    def ids(k, src, dst, device):
        return send(src, dst, id_s.at[k], id_r.at[k], device)

    id_x = [ids(i, idt.at[0], idt.at[4 + 2 * x_lo + i], x_near[i]) for i in range(2)]
    id_f = ids(2, idt.at[6 - 2 * x_lo], idt.at[1], x_near[1])
    id_z = ids(3, idt.at[6:8], idt.at[4:6], z_up)
    id_o = ids(4, idt.at[pl.ds(4 * core, 2)], idt.at[2:4], other)
    id_y = [ids(5 + i, idi.at[0], idi.at[1 + i], y_near[i]) for i in range(2)]
    id_h = ids(7, idi.at[1], idi.at[3], y_near[0])

    loads[0].wait()
    normalize(raw_t, txt)
    loads[2].wait()
    loads[3].wait()
    pl.semaphore_wait(barrier, 6)
    for i in range(2):
        gx(i).start()

    @pl.when(low)
    def _():
        for i in range(2):
            g2(i).start()

    @pl.when(high)
    def _():
        for i in range(2):
            gz(i).start()

    loads[1].wait()
    normalize(raw_i, img)
    for i in range(2):
        gy(i).start()
    for i in range(2):
        gw(i).start()
    for copy in id_x + id_y:
        copy.start()

    @pl.when(core == 0)
    def _():
        go(0).start()

    for i in range(2):
        gx(i).wait_recv()
        gf(i).start()

        @pl.when(low)
        def _():
            gz(i).start()

    for i in range(2):
        gy(i).wait_recv()
        gh(i).start()

    @pl.when(high)
    def _():
        for i in range(2):
            gz(i).wait_recv()
            g2(1 - i).start()

    for copy in id_x + id_y:
        copy.wait_recv()
    id_f.start()
    id_h.start()

    @pl.when(low)
    def _():
        id_z.start()
        id_z.wait_recv()

    id_f.wait_recv()
    id_o.start()

    for i in range(2):
        gw(i).wait_recv()
    for i in range(2):
        g2(i).wait_recv()

        @pl.when(low)
        def _():
            gz(i).wait_recv()

        @pl.when(core == 1)
        def _():
            go(i).start()

    for i in range(2):
        gf(i).wait_recv()

    @pl.when(core == 0)
    def _():
        go(1).start()

    id_h.wait_recv()
    for s in range(4):
        keys[s * R:(s + 1) * R, :] = jnp.transpose(jnp.broadcast_to(idi[s], (128, R)))
    id_o.wait_recv()
    for i in range(2):
        gh(i).wait_recv()

    scale_value, bias_value = scale[0], bias[0]

    def weigh(b):
        def body(a, carry):
            rows = pl.ds(pl.multiple_of(a * 2 * R, 2 * R), 2 * R)
            dots = lax.dot_general(
                img[rows, :], txt[b * 2 * R:(b + 1) * 2 * R, :], (((1,), (1,)), ((), ())), preferred_element_type=F32)
            logits = scale_value * dots + bias_value
            mine = keys[rows, :]
            same = jnp.concatenate([mine == idt[2 * b], mine == idt[2 * b + 1]], axis=1)
            share = jax.nn.sigmoid(jnp.where(same, -logits, logits))
            weights = jnp.where(same, -share, share)
            w[rows, b * 2 * R:(b + 1) * 2 * R] = weights.astype(BF16)
            wt[b * 2 * R:(b + 1) * 2 * R, rows] = jnp.transpose(weights).astype(BF16)
            return carry

        lax.fori_loop(0, 2, body, 0)

    weigh(0)
    weigh(2)
    for i in range(2):
        go(i).wait_recv()
    weigh(1)

    def ro(i):
        return send(block(oc_s, i), block(oc_r, i), ro_s.at[i], ro_r.at[i], other)

    def rd(i):
        return send(half(d_s, 0, i), half(d_r, 0, i), rd_s.at[i], rd_r.at[i], x_near[1 - i])

    def rc(i):
        return send(half(c_s, i, 1 - i), half(c_r, 0, 1 - i), rc_s.at[i], rc_r.at[i], x_near[i])

    def rz(i):
        return send(half(c_s, i, i), half(z_r, 0, i), rz_s.at[i], rz_r.at[i], z_down)

    def rz_on(i):
        return send(half(c_r, 0, i), half(z_r, 0, i), rz_s.at[i], rz_r.at[i], z_down)

    def rx(i):
        return send(half(x_s, 0, i), half(x_r, 0, i), rx_s.at[i], rx_r.at[i], x_near[i])

    def rh(i):
        return send(half(h_s, 0, i), half(h_r, 0, i), rh_s.at[i], rh_r.at[i], y_near[i])

    def rn(i):
        return send(half(y_s, i, 1 - i), half(y_r, i, 1 - i), rn_s.at[i], rn_r.at[i], y_near[i])

    def ra(i):
        return send(half(y_s, i, i), half(y_r, i, i), ra_s.at[i], ra_r.at[i], y_near[i])

    def text_part(b, store):
        def body(n, carry):
            cols = pl.ds(pl.multiple_of(n * TILE, TILE), TILE)
            rows = pl.ds(b * 2 * R if isinstance(b, int) else pl.multiple_of(b * 2 * R, 2 * R), 2 * R)
            store(cols, jnp.dot(wt[rows, :], img[:, cols], preferred_element_type=F32))
            return carry

        lax.fori_loop(0, D // TILE, body, 0)

    def image_part(a, store):
        def body(n, carry):
            cols = pl.ds(pl.multiple_of(n * TILE, TILE), TILE)
            store(cols, jnp.dot(w[a * 2 * R:(a + 1) * 2 * R, :], txt[0:6 * R, cols], preferred_element_type=F32))
            return carry

        lax.fori_loop(0, D // TILE, body, 0)

    def keep_other(cols, part):
        oc_s[:, cols] = part.astype(BF16)

    text_part(1, keep_other)
    for i in range(2):
        ro(i).start()

    def keep_far(cols, part):
        h_s[:, cols] = part[R:2 * R].astype(BF16)
        gi[2 * R:3 * R, cols] = part[0:R]
        y_s[H:R, cols] = part[H:R].astype(BF16)

    image_part(1, keep_far)
    for i in range(2):
        rh(i).start()
    rn(0).start()

    def keep_near(cols, part):
        gi[0:2 * R, cols] = part
        y_s[R:R + H, cols] = part[R:R + H].astype(BF16)

    image_part(0, keep_near)
    rn(1).start()

    def keep_text(b):
        def store(cols, part):
            gt[pl.ds(pl.multiple_of(b * 2 * R, 2 * R), 2 * R), cols] = part

        return store

    text_part(2 * (1 - core), keep_text(1 - core))
    text_part(2 * core, keep_text(core))
    for i in range(2):
        ro(i).wait_recv()
    at = pl.ds(pl.multiple_of(core * 2 * R, 2 * R), 2 * R)
    gt[at, :] = gt[at, :] + oc_r[...].astype(F32)
    c_s[...] = gt[2 * R:4 * R, :].astype(BF16)
    for i in range(2):
        rc(i).start()

    @pl.when(low)
    def _():
        for i in range(2):
            rz(i).start()

    d_s[...] = gt[R:2 * R, :].astype(BF16)
    for i in range(2):
        rd(i).start()

    for i in range(2):
        rh(i).wait_recv()
        y_s[i * R + i * H:i * R + (i + 1) * H, :] = (
            gi[(2 - i) * R + i * H:(2 - i) * R + (i + 1) * H, :] + h_r[i * H:(i + 1) * H, :].astype(F32)).astype(BF16)
        ra(i).start()

    for i in range(2):
        rc(i).wait_recv()

    @pl.when(high)
    def _():
        for i in range(2):
            rz_on(i).start()

    @pl.when(low)
    def _():
        for i in range(2):
            rz(i).wait_recv()
            gt[(2 + i) * R + i * H:(2 + i) * R + (i + 1) * H, :] = z_r[i * H:(i + 1) * H, :].astype(F32)

    for i in range(2):
        rd(i).wait_recv()
        x_s[i * H:(i + 1) * H, :] = (
            gt[(2 + i) * R + i * H:(2 + i) * R + (i + 1) * H, :] + d_r[i * H:(i + 1) * H, :].astype(F32)).astype(BF16)
        rx(i).start()

    def backward(rows, total, out):
        values = rows[...].astype(F32)
        factor = 1.0 / jnp.sqrt(jnp.sum(values * values, axis=-1, keepdims=True) + epsilon)
        unit = values * factor
        grad = scale_value * total
        along = jnp.sum(unit * grad, axis=-1, keepdims=True)
        out[...] = factor * (grad - unit * along)

    for i in range(2):
        rn(i).wait_recv()
        ra(i).wait_recv()
    backward(raw_i, gi[0:R, :] + (y_r[0:R, :].astype(F32) + y_r[R:2 * R, :].astype(F32)), image_out)

    @pl.when(high)
    def _():
        for i in range(2):
            rz(i).wait_recv()
        gt[R:2 * R, :] = gt[0:R, :] + z_r[...].astype(F32)

    @pl.when(low)
    def _():
        gt[R:2 * R, :] = gt[0:R, :] + c_r[...].astype(F32)

    for i in range(2):
        rx(i).wait_recv()
    backward(raw_t, gt[R:2 * R, :] + x_r[...].astype(F32), text_out)

    for i in range(2):
        for copy in (gx, g2, gf, gz, go, gy, gw, gh, ro, rd, rc, rz, rx, rh, rn, ra):
            copy(i).wait_send()
    for copy in id_x + id_y + [id_f, id_o, id_h]:
        copy.wait_send()

    @pl.when(low)
    def _():
        id_z.wait_send()


def shards(n_loop, images, texts, image_ids, text_ids, logit_scale, logit_bias):
    R, D = images.shape
    dma = pltpu.SemaphoreType.DMA
    vmem = pl.BlockSpec(memory_space=pltpu.VMEM)
    smem = pl.BlockSpec(memory_space=pltpu.SMEM)
    anywhere = pl.BlockSpec(memory_space=pl.ANY)

    def rows(count, dtype=BF16):
        return pltpu.VMEM((count * R, D), dtype)

    return pl.pallas_call(
        functools.partial(kernel, n_loop),
        out_shape=(jax.ShapeDtypeStruct((R, D), F32), jax.ShapeDtypeStruct((R, D), F32)),
        in_specs=[anywhere, anywhere, anywhere, anywhere, smem, smem],
        out_specs=(vmem, vmem),
        scratch_shapes=[
            rows(1), rows(1), rows(4), rows(8),
            pltpu.VMEM((4, 1, R), jnp.int32), pltpu.VMEM((8, 1, R), jnp.int32), pltpu.VMEM((4 * R, 128), jnp.int32),
            pltpu.VMEM((4 * R, 6 * R), BF16), pltpu.VMEM((6 * R, 4 * R), BF16), rows(4, F32), rows(3, F32),
            rows(2), rows(2), rows(1), rows(1), rows(2), rows(1), rows(1), rows(1), rows(1), rows(1), rows(1),
            rows(2), rows(2), dma((4,)),
        ] + [dma((2,))] * 16 + [dma((8,))] * 2 + [dma((2,))] * 16,
        compiler_params=pltpu.CompilerParams(
            collective_id=0, has_side_effects=True, vmem_limit_bytes=56 * 1024 * 1024),
        cost_estimate=pl.CostEstimate(
            flops=6 * 4 * R * 6 * R * D, bytes_accessed=12 * R * D, transcendentals=24 * R * R),
    )(images, texts, image_ids.reshape(1, R), text_ids.reshape(1, R), logit_scale, logit_bias)


def solution(mesh):
    rows = P(("loop", "group"), None)
    ids = P(("loop", "group"))
    return jax.shard_map(
        functools.partial(shards, mesh.shape["loop"]), mesh=mesh,
        in_specs=(rows, rows, ids, ids, P(), P()), out_specs=(rows, rows), check_vma=False)
```

time: 399 us -> 57.6 us (0.14)
  waiting for transfers between devices: 301 us -> 0 us
  Pallas kernels: 0 us -> 52.7 us
  blocking collectives: 39.2 us -> 0 us
  starting transfers between devices: 20.7 us -> 0 us
  between operations: 15.5 us -> 1.94 us
  other arithmetic: 11 us -> 0 us
  matrix products: 8.4 us -> 0 us
    ppermute x6 -> x0, waiting for transfers between devices: 127 us -> none  [from_behind(): return lax.ppermute(value, axis, pairs)]
    reduce_scatter x1 -> x0, waiting for transfers between devices: 96.8 us -> none  [shards(): lax.psum_scatter(carried_sum, 'group', scatter_dimension=0, tiled=True)]
    all_gather x1 -> x0, waiting for transfers between devices: 77.9 us -> none  [shards(): lax.all_gather(text_unit, 'group', axis=0, tiled=True)]
    pallas_call x0 -> x1, Pallas kernels: none -> 52.7 us  [shards(): pl.pallas_call(functools.partial(kernel, n_loop), out_shape=(jax.ShapeDty...]
    all_gather x1 -> x0, blocking collectives: 39.2 us -> none  [shards(): lax.all_gather(text_ids, 'group', axis=0, tiled=True)]
    ppermute x6 -> x0, starting transfers between devices: 20.6 us -> none  [from_behind(): return lax.ppermute(value, axis, pairs)]
    dot_general x9 -> x0, matrix products: 8.4 us -> none  [the longest x3 4.21 us: pair_terms(): lax.dot_general(image_block, text_block, (((1,), (1,)), ((), ())), prefer...]
  transfers between devices with their start and end apart: 8 -> 0, of which waited for: 5 -> 0; matrix products, arithmetic and copies ran while one was open for 2% -> 0% of each run, Pallas kernels for 0% -> 0%
where the time goes in v2:
time: 57.6 us; the launch traced here: 57.4 us
  Pallas kernels  52.7 us (91%)
  local copies, waits for them, and re-layouts  2.8 us (5%)
  between operations  1.94 us (3%)
    pallas_call x1, Pallas kernels, shards(): pl.pallas_call(functools.partial(kernel, n_loop), out_shape=(jax.ShapeDty...  52.7 us
    unnamed x4, local copies, waits for them, and re-layouts  2.8 us

profile of v2, /device:TPU:1, one launch (start us, length us, event | category | flops | bytes accessed | tf_op | source)
XLA Modules:
  0.0 57.4 jit_solution(2025857002495811840)
XLA Ops:
  1.9 52.7 %shard_map.77 = (f32[128,1152]{1,0:T(8,128)}, f32[128,1152]{1,0:T(8,128)}) custom-call(bf16[128,1152]{1,0:T(8,128)(2,1)} %images.1, bf16[128,1152]{1,0:T(8,128)(2,1)} %texts.1, s32[1,128]{1,0:T(1,128)} %bitcast.2, s32[1,128]{1,0:T(1,128)} %bitcast.3, f32[1]{0:T(128)S(6)} %copy.10.scale, f32[1]{0:T(128)S(6)} %copy.11.bias), custom_call_target="tpu_custom_call" | custom-call | flops 2717908992 | bytes 1769472 | tf_op jit(solution)/shard_map/pallas_call | solution.py:380
  54.6 0.0 copy-start
  54.6 2.0 %copy.12 = f32[128,1152]{1,0:T(8,128)} copy(f32[128,1152]{1,0:T(8,128)} %get-tuple-element.4) | data formatting | bytes 1179648
  56.6 0.0 copy-done
  56.6 0.8 %copy.13 = f32[128,1152]{1,0:T(8,128)} copy(f32[128,1152]{1,0:T(8,128)S(1)} %copy-done) | data formatting | bytes 1179648
Async XLA Ops:
  54.6 2.0 %copy-start = (f32[128,1152]{1,0:T(8,128)S(1)}, f32[128,1152]{1,0:T(8,128)}, u32[]{:S(2)}) copy-start(f32[128,1152]{1,0:T(8,128)} %get-tuple-element.5) | copy-start | bytes 1769476

commit v3 on v2

--- a/solution.py
+++ b/solution.py
@@ -10,13 +10,13 @@
 epsilon = 1e-06
 MESH = pl.DeviceIdType.MESH
 F32, BF16 = jnp.float32, jnp.bfloat16
-TILE = 384
+ROWS_AT_ONCE = 256
 
 
 def kernel(
     n_loop, images, texts, image_ids, text_ids, scale, bias, image_out, text_out,
     raw_i, raw_t, img, txt, idi, idt, keys, w, wt, gt, gi,
-    oc_s, oc_r, d_s, d_r, c_s, c_r, z_r, x_s, x_r, h_s, h_r, y_s, y_r,
+    t_s, oc_r, d_s, d_r, c_r, z_r, x_s, x_r, h_s, h_r, y_s, y_r,
     load, gx_s, gx_r, g2_s, g2_r, gf_s, gf_r, gz_s, gz_r, go_s, go_r, gy_s, gy_r, gw_s, gw_r, gh_s, gh_r, id_s, id_r,
     ro_s, ro_r, rd_s, rd_r, rc_s, rc_r, rz_s, rz_r, rx_s, rx_r, rh_s, rh_r, rn_s, rn_r, ra_s, ra_r,
 ):
@@ -154,24 +154,24 @@
     @pl.when(low)
     def _():
         id_z.start()
-        id_z.wait_recv()
 
     id_f.wait_recv()
-    id_o.start()
+
+    @pl.when(high | (core == 0))
+    def _():
+        id_o.start()
+
+    @pl.when(high)
+    def _():
+        for i in range(2):
+            g2(i).wait_recv()
+
+            @pl.when(core == 1)
+            def _():
+                go(i).start()
 
     for i in range(2):
         gw(i).wait_recv()
-    for i in range(2):
-        g2(i).wait_recv()
-
-        @pl.when(low)
-        def _():
-            gz(i).wait_recv()
-
-        @pl.when(core == 1)
-        def _():
-            go(i).start()
-
     for i in range(2):
         gf(i).wait_recv()
 
@@ -182,45 +182,38 @@
     id_h.wait_recv()
     for s in range(4):
         keys[s * R:(s + 1) * R, :] = jnp.transpose(jnp.broadcast_to(idi[s], (128, R)))
-    id_o.wait_recv()
     for i in range(2):
         gh(i).wait_recv()
 
     scale_value, bias_value = scale[0], bias[0]
 
+    def pair(b):
+        return pl.ds(b * 2 * R if isinstance(b, int) else pl.multiple_of(b * 2 * R, 2 * R), 2 * R)
+
     def weigh(b):
-        def body(a, carry):
-            rows = pl.ds(pl.multiple_of(a * 2 * R, 2 * R), 2 * R)
+        for a in range(4 * R // ROWS_AT_ONCE):
+            rows = slice(a * ROWS_AT_ONCE, (a + 1) * ROWS_AT_ONCE)
             dots = lax.dot_general(
-                img[rows, :], txt[b * 2 * R:(b + 1) * 2 * R, :], (((1,), (1,)), ((), ())), preferred_element_type=F32)
+                img[rows, :], txt[pair(b), :], (((1,), (1,)), ((), ())), preferred_element_type=F32)
             logits = scale_value * dots + bias_value
             mine = keys[rows, :]
             same = jnp.concatenate([mine == idt[2 * b], mine == idt[2 * b + 1]], axis=1)
             share = jax.nn.sigmoid(jnp.where(same, -logits, logits))
             weights = jnp.where(same, -share, share)
-            w[rows, b * 2 * R:(b + 1) * 2 * R] = weights.astype(BF16)
-            wt[b * 2 * R:(b + 1) * 2 * R, rows] = jnp.transpose(weights).astype(BF16)
-            return carry
-
-        lax.fori_loop(0, 2, body, 0)
-
-    weigh(0)
-    weigh(2)
-    for i in range(2):
-        go(i).wait_recv()
-    weigh(1)
+            w[rows, pair(b)] = weights.astype(BF16)
+            wt[pair(b), rows] = jnp.transpose(weights).astype(BF16)
 
     def ro(i):
-        return send(block(oc_s, i), block(oc_r, i), ro_s.at[i], ro_r.at[i], other)
+        return send(block(t_s, i), block(oc_r, i), ro_s.at[i], ro_r.at[i], other)
 
     def rd(i):
         return send(half(d_s, 0, i), half(d_r, 0, i), rd_s.at[i], rd_r.at[i], x_near[1 - i])
 
     def rc(i):
-        return send(half(c_s, i, 1 - i), half(c_r, 0, 1 - i), rc_s.at[i], rc_r.at[i], x_near[i])
+        return send(half(t_s, 2 + i, 1 - i), half(c_r, 0, 1 - i), rc_s.at[i], rc_r.at[i], x_near[i])
 
     def rz(i):
-        return send(half(c_s, i, i), half(z_r, 0, i), rz_s.at[i], rz_r.at[i], z_down)
+        return send(half(t_s, 2 + i, i), half(z_r, 0, i), rz_s.at[i], rz_r.at[i], z_down)
 
     def rz_on(i):
         return send(half(c_r, 0, i), half(z_r, 0, i), rz_s.at[i], rz_r.at[i], z_down)
@@ -237,71 +230,102 @@
     def ra(i):
         return send(half(y_s, i, i), half(y_r, i, i), ra_s.at[i], ra_r.at[i], y_near[i])
 
-    def text_part(b, store):
-        def body(n, carry):
-            cols = pl.ds(pl.multiple_of(n * TILE, TILE), TILE)
-            rows = pl.ds(b * 2 * R if isinstance(b, int) else pl.multiple_of(b * 2 * R, 2 * R), 2 * R)
-            store(cols, jnp.dot(wt[rows, :], img[:, cols], preferred_element_type=F32))
-            return carry
-
-        lax.fori_loop(0, D // TILE, body, 0)
-
-    def image_part(a, store):
-        def body(n, carry):
-            cols = pl.ds(pl.multiple_of(n * TILE, TILE), TILE)
-            store(cols, jnp.dot(w[a * 2 * R:(a + 1) * 2 * R, :], txt[0:6 * R, cols], preferred_element_type=F32))
-            return carry
-
-        lax.fori_loop(0, D // TILE, body, 0)
-
-    def keep_other(cols, part):
-        oc_s[:, cols] = part.astype(BF16)
-
-    text_part(1, keep_other)
-    for i in range(2):
-        ro(i).start()
-
-    def keep_far(cols, part):
-        h_s[:, cols] = part[R:2 * R].astype(BF16)
-        gi[2 * R:3 * R, cols] = part[0:R]
-        y_s[H:R, cols] = part[H:R].astype(BF16)
-
-    image_part(1, keep_far)
+    def text_part(b):
+        return jnp.dot(wt[pair(b), :], img[...], preferred_element_type=F32)
+
+    def image_part(a):
+        return jnp.dot(w[a * 2 * R:(a + 1) * 2 * R, :], txt[0:6 * R, :], preferred_element_type=F32)
+
+    def send_far():
+        d_s[...] = gt[R:2 * R, :].astype(BF16)
+        for i in range(2):
+            rd(i).start()
+
+    def send_cross():
+        for i in range(2):
+            rc(i).start()
+
+        @pl.when(low)
+        def _():
+            for i in range(2):
+                rz(i).start()
+
+    weigh(0)
+    gt[0:2 * R, :] = text_part(0)
+    pl.when(core == 1)(send_far)
+
+    @pl.when(low)
+    def _():
+        id_z.wait_recv()
+
+        @pl.when(core == 1)
+        def _():
+            id_o.start()
+
+        for i in range(2):
+            g2(i).wait_recv()
+            gz(i).wait_recv()
+
+            @pl.when(core == 1)
+            def _():
+                go(i).start()
+
+    @pl.when(core == 1)
+    def _():
+        id_o.wait_recv()
+        for i in range(2):
+            go(i).wait_recv()
+
+    weigh(2 - core)
+    t_s[pair(1 - core), :] = text_part(2 - core).astype(BF16)
+
+    @pl.when(core == 1)
+    def _():
+        for i in range(2):
+            ro(i).start()
+
+    pl.when(core == 0)(send_cross)
+
+    @pl.when(core == 0)
+    def _():
+        id_o.wait_recv()
+        for i in range(2):
+            go(i).wait_recv()
+
+    weigh(1 + core)
+    gt[2 * R:4 * R, :] = text_part(1 + core)
+
+    @pl.when(core == 0)
+    def _():
+        t_s[0:2 * R, :] = gt[2 * R:4 * R, :].astype(BF16)
+        for i in range(2):
+            ro(i).start()
+
+    part = image_part(1)
+    h_s[...] = part[R:2 * R].astype(BF16)
+    gi[2 * R:3 * R, :] = part[0:R]
+    y_s[H:R, :] = part[H:R].astype(BF16)
     for i in range(2):
         rh(i).start()
     rn(0).start()
 
-    def keep_near(cols, part):
-        gi[0:2 * R, cols] = part
-        y_s[R:R + H, cols] = part[R:R + H].astype(BF16)
-
-    image_part(0, keep_near)
+    for i in range(2):
+        ro(i).wait_recv()
+
+    @pl.when(core == 0)
+    def _():
+        gt[0:2 * R, :] = gt[0:2 * R, :] + oc_r[...].astype(F32)
+        send_far()
+
+    @pl.when(core == 1)
+    def _():
+        t_s[2 * R:4 * R, :] = (gt[2 * R:4 * R, :] + oc_r[...].astype(F32)).astype(BF16)
+        send_cross()
+
+    part = image_part(0)
+    gi[0:2 * R, :] = part
+    y_s[R:R + H, :] = part[R:R + H].astype(BF16)
     rn(1).start()
-
-    def keep_text(b):
-        def store(cols, part):
-            gt[pl.ds(pl.multiple_of(b * 2 * R, 2 * R), 2 * R), cols] = part
-
-        return store
-
-    text_part(2 * (1 - core), keep_text(1 - core))
-    text_part(2 * core, keep_text(core))
-    for i in range(2):
-        ro(i).wait_recv()
-    at = pl.ds(pl.multiple_of(core * 2 * R, 2 * R), 2 * R)
-    gt[at, :] = gt[at, :] + oc_r[...].astype(F32)
-    c_s[...] = gt[2 * R:4 * R, :].astype(BF16)
-    for i in range(2):
-        rc(i).start()
-
-    @pl.when(low)
-    def _():
-        for i in range(2):
-            rz(i).start()
-
-    d_s[...] = gt[R:2 * R, :].astype(BF16)
-    for i in range(2):
-        rd(i).start()
 
     for i in range(2):
         rh(i).wait_recv()
@@ -317,23 +341,28 @@
         for i in range(2):
             rz_on(i).start()
 
-    @pl.when(low)
-    def _():
-        for i in range(2):
+    def send_near(i, first):
+        at = slice(i * H, (i + 1) * H)
+        x_s[at, :] = (first.astype(F32) + d_r[at, :].astype(F32)).astype(BF16)
+        rx(i).start()
+
+    for i in range(2):
+        rd(i).wait_recv()
+
+        @pl.when(low)
+        def _():
             rz(i).wait_recv()
-            gt[(2 + i) * R + i * H:(2 + i) * R + (i + 1) * H, :] = z_r[i * H:(i + 1) * H, :].astype(F32)
-
-    for i in range(2):
-        rd(i).wait_recv()
-        x_s[i * H:(i + 1) * H, :] = (
-            gt[(2 + i) * R + i * H:(2 + i) * R + (i + 1) * H, :] + d_r[i * H:(i + 1) * H, :].astype(F32)).astype(BF16)
-        rx(i).start()
+            send_near(i, z_r[i * H:(i + 1) * H, :])
+
+        @pl.when(high)
+        def _():
+            send_near(i, t_s[(2 + i) * R + i * H:(2 + i) * R + (i + 1) * H, :])
 
     def backward(rows, total, out):
         values = rows[...].astype(F32)
         factor = 1.0 / jnp.sqrt(jnp.sum(values * values, axis=-1, keepdims=True) + epsilon)
         unit = values * factor
-        grad = scale_value * total
+        grad = total
         along = jnp.sum(unit * grad, axis=-1, keepdims=True)
         out[...] = factor * (grad - unit * along)
 
@@ -372,12 +401,12 @@
     dma = pltpu.SemaphoreType.DMA
     vmem = pl.BlockSpec(memory_space=pltpu.VMEM)
     smem = pl.BlockSpec(memory_space=pltpu.SMEM)
-    anywhere = pl.BlockSpec(memory_space=pl.ANY)
+    anywhere = pl.BlockSpec(memory_space=pltpu.HBM)
 
     def rows(count, dtype=BF16):
         return pltpu.VMEM((count * R, D), dtype)
 
-    return pl.pallas_call(
+    image_rows, text_rows = pl.pallas_call(
         functools.partial(kernel, n_loop),
         out_shape=(jax.ShapeDtypeStruct((R, D), F32), jax.ShapeDtypeStruct((R, D), F32)),
         in_specs=[anywhere, anywhere, anywhere, anywhere, smem, smem],
@@ -386,7 +415,7 @@
             rows(1), rows(1), rows(4), rows(8),
             pltpu.VMEM((4, 1, R), jnp.int32), pltpu.VMEM((8, 1, R), jnp.int32), pltpu.VMEM((4 * R, 128), jnp.int32),
             pltpu.VMEM((4 * R, 6 * R), BF16), pltpu.VMEM((6 * R, 4 * R), BF16), rows(4, F32), rows(3, F32),
-            rows(2), rows(2), rows(1), rows(1), rows(2), rows(1), rows(1), rows(1), rows(1), rows(1), rows(1),
+            rows(4), rows(2), rows(1), rows(1), rows(1), rows(1), rows(1), rows(1), rows(1), rows(1),
             rows(2), rows(2), dma((4,)),
         ] + [dma((2,))] * 16 + [dma((8,))] * 2 + [dma((2,))] * 16,
         compiler_params=pltpu.CompilerParams(
@@ -394,6 +423,7 @@
         cost_estimate=pl.CostEstimate(
             flops=6 * 4 * R * 6 * R * D, bytes_accessed=12 * R * D, transcendentals=24 * R * R),
     )(images, texts, image_ids.reshape(1, R), text_ids.reshape(1, R), logit_scale, logit_bias)
+    return image_rows * logit_scale[0], text_rows * logit_scale[0]
 
 
 def solution(mesh):

time: 57.6 us -> 48.6 us (0.84)
  Pallas kernels: 52.7 us -> 44.2 us
  local copies, waits for them, and re-layouts: 2.8 us -> 0 us
  other arithmetic: 0 us -> 2.33 us
    pallas_call x1, Pallas kernels: 52.7 us -> 44.2 us  [shards(): pl.pallas_call(functools.partial(kernel, n_loop), out_shape=(jax.ShapeDty...]
    unnamed x4 -> x0, local copies, waits for them, and re-layouts: 2.8 us -> none
    mul x0 -> x1, other arithmetic: none -> 2.33 us  [shards(): return (image_rows * logit_scale[0], text_rows * logit_scale[0])]
where the time goes in v3:
time: 48.6 us; the launch traced here: 48.4 us
  Pallas kernels  44.2 us (91%)
  other arithmetic  2.33 us (5%)
  between operations  1.93 us (4%)
    pallas_call x1, Pallas kernels, shards(): pl.pallas_call(functools.partial(kernel, n_loop), out_shape=(jax.ShapeDty...  44.2 us
    mul x1, other arithmetic, shards(): return (image_rows * logit_scale[0], text_rows * logit_scale[0])  2.33 us

profile of v3, /device:TPU:1, one launch (start us, length us, event | category | flops | bytes accessed | tf_op | source)
XLA Modules:
  0.0 48.4 jit_solution(1390458041712738984)
XLA Ops:
  1.9 44.2 %shard_map.77 = (f32[128,1152]{1,0:T(8,128)}, f32[128,1152]{1,0:T(8,128)}) custom-call(bf16[128,1152]{1,0:T(8,128)(2,1)} %images.1, bf16[128,1152]{1,0:T(8,128)(2,1)} %texts.1, s32[1,128]{1,0:T(1,128)} %bitcast.4, s32[1,128]{1,0:T(1,128)} %bitcast.5, f32[1]{0:T(128)} %copy.8.scale, f32[1]{0:T(128)S(6)} %copy.9.bias), custom_call_target="tpu_custom_call" | custom-call | flops 2717908992 | bytes 1769472 | tf_op jit(solution)/shard_map/pallas_call | solution.py:409
  46.1 2.3 %broadcast_multiply_fusion = (f32[128,1152]{1,0:T(8,128)}, f32[128,1152]{1,0:T(8,128)}) fusion(f32[128,1152]{1,0:T(8,128)} %get-tuple-element.5, f32[]{:T(128)} %bitcast.3, f32[128,1152]{1,0:T(8,128)} %get-tuple-element.4), kind=kLoop, calls=%fused_computation | loop fusion | flops 294912 | bytes 2359300 | tf_op jit(solution)/shard_map/mul | solution.py:426

commit v4 on v3

v4 whole, which is shorter than its diff:
```python
import functools

import jax
import jax.numpy as jnp
from jax import lax
from jax.experimental import pallas as pl
from jax.experimental.pallas import tpu as pltpu
from jax.sharding import PartitionSpec as P

epsilon = 1e-06
MESH = pl.DeviceIdType.MESH
F32, BF16 = jnp.float32, jnp.bfloat16
ROWS_AT_ONCE = 256
PIECES = 2
PARTS = 2


def kernel(
    n_loop, images, texts, image_ids, text_ids, scale, bias, image_out, text_out,
    raw_i, raw_t, img, txt, idi, idt, keys, w, wt, gt, gi,
    t_s, oc_r, d_s, d_r, c_r, z_r, x_s, x_r, h_s, h_r, y_s, y_r,
    load, gx_s, gx_r, g2_s, g2_r, gf_s, gf_r, gz_s, gz_r, go_s, go_r, gy_s, gy_r, gw_s, gw_r, gh_s, gh_r, id_s, id_r,
    ro_s, ro_r, rd_s, rd_r, rc_s, rc_r, rz_s, rz_r, rx_s, rx_r, rh_s, rh_r, rn_s, rn_r, ra_s, ra_r,
):
    R, D = raw_i.shape
    H = R // 2
    loop, group = lax.axis_index("loop"), lax.axis_index("group")
    core = lax.rem(loop, 2)
    x_lo = lax.rem(loop // 2, 2)
    y, x_hi = group // 2, lax.rem(group, 2)
    flip = loop + 2 - 4 * x_lo
    other = (loop + 1 - 2 * core, group)
    x_near = ((flip, group), (flip, group + 1 - 2 * x_hi))
    y_near = ((loop, lax.rem(y + 1, 4) * 2 + x_hi), (loop, lax.rem(y + 3, 4) * 2 + x_hi))
    z_up = (lax.rem(loop + 4, n_loop), group)
    z_down = (lax.rem(loop + n_loop - 4, n_loop), group)
    low, high = x_lo == 0, x_lo == 1

    loads = [
        pltpu.make_async_copy(src, dst, load.at[i])
        for i, (src, dst) in enumerate(
            [(texts, raw_t), (images, raw_i), (text_ids, idt.at[0]), (image_ids, idi.at[0])])
    ]
    for copy in loads:
        copy.start()
    barrier = pltpu.get_barrier_semaphore()
    for device in (*x_near, *y_near, z_down, other):
        pl.semaphore_signal(barrier, inc=1, device_id=device, device_id_type=MESH)

    def normalize(rows, block):
        values = rows[...].astype(F32)
        factor = 1.0 / jnp.sqrt(jnp.sum(values * values, axis=-1, keepdims=True) + epsilon)
        block[0:R, :] = (values * factor).astype(BF16)

    def send(src, dst, s, r, device):
        return pltpu.make_async_remote_copy(
            src_ref=src, dst_ref=dst, send_sem=s, recv_sem=r, device_id=device, device_id_type=MESH)

    def half(ref, slot, h, q, count):
        size = H // count
        at = slot * R + h * H + q * size
        return ref.at[pl.ds(at if isinstance(at, int) else pl.multiple_of(at, size), size)]

    def block(ref, slot):
        at = slot * R
        return ref.at[pl.ds(at if isinstance(at, int) else pl.multiple_of(at, R), R)]

    def gx(i, q):
        return send(half(txt, 0, i, q, PIECES), half(txt, 4 + 2 * x_lo + i, i, q, PIECES), gx_s.at[i, q], gx_r.at[i, q], x_near[i])

    def g2(i, q):
        return send(half(txt, 6 * x_lo, 1 - i, q, PIECES), half(txt, 4 + i, 1 - i, q, PIECES), g2_s.at[i, q], g2_r.at[i, q], x_near[i])

    def gf(i, q):
        return send(half(txt, 6 - 2 * x_lo + i, i, q, PIECES), half(txt, 1, i, q, PIECES), gf_s.at[i, q], gf_r.at[i, q], x_near[1 - i])

    def gz(i, q):
        return send(half(txt, (6 + i) * (1 - x_lo), i, q, PIECES), half(txt, 4 + i + x_lo * (2 - i), i, q, PIECES),
                    gz_s.at[i, q], gz_r.at[i, q], z_up)

    def go(i, h):
        return send(half(txt, 4 * core + i, h, 0, 1), half(txt, 2 + i, h, 0, 1), go_s.at[i, h], go_r.at[i, h], other)

    def gy(i, q):
        return send(half(img, 0, i, q, PIECES), half(img, 1 + i, i, q, PIECES), gy_s.at[i, q], gy_r.at[i, q], y_near[i])

    def gw(i, q):
        return send(half(img, 0, 1 - i, q, PIECES), half(img, 1 + i, 1 - i, q, PIECES), gw_s.at[i, q], gw_r.at[i, q], y_near[i])

    def gh(i, q):
        return send(half(img, 1 + i, i, q, PIECES), half(img, 3, i, q, PIECES), gh_s.at[i, q], gh_r.at[i, q], y_near[i])

    def ids(k, src, dst, device):
        return send(src, dst, id_s.at[k], id_r.at[k], device)

    id_x = [ids(i, idt.at[0], idt.at[4 + 2 * x_lo + i], x_near[i]) for i in range(2)]
    id_f = ids(2, idt.at[6 - 2 * x_lo], idt.at[1], x_near[1])
    id_z = ids(3, idt.at[6:8], idt.at[4:6], z_up)
    id_o = ids(4, idt.at[pl.ds(4 * core, 2)], idt.at[2:4], other)
    id_y = [ids(5 + i, idi.at[0], idi.at[1 + i], y_near[i]) for i in range(2)]
    id_h = ids(7, idi.at[1], idi.at[3], y_near[0])

    def pieces(count):
        return [(i, q) for q in range(count) for i in range(2)]

    loads[0].wait()
    normalize(raw_t, txt)
    loads[2].wait()
    loads[3].wait()
    pl.semaphore_wait(barrier, 6)
    for copy in id_x + id_y:
        copy.start()
    for i, q in pieces(PIECES):
        gx(i, q).start()

    @pl.when(low)
    def _():
        for i, q in pieces(PIECES):
            g2(i, q).start()

    @pl.when(high)
    def _():
        for i, q in pieces(PIECES):
            gz(i, q).start()

    loads[1].wait()
    normalize(raw_i, img)
    for i, q in pieces(PIECES):
        gy(i, q).start()
    for i, q in pieces(PIECES):
        gw(i, q).start()

    @pl.when(core == 0)
    def _():
        for h in range(2):
            go(0, h).start()

    for copy in id_x + id_y:
        copy.wait_recv()
    id_f.start()
    id_h.start()

    @pl.when(low)
    def _():
        id_z.start()

    for q in range(PIECES):
        for i in range(2):
            gx(i, q).wait_recv()
            gf(i, q).start()

            @pl.when(low)
            def _():
                gz(i, q).start()

        for i in range(2):
            gy(i, q).wait_recv()
            gh(i, q).start()

    def pass_sideways(q):
        for i in range(2):
            gz(i, q).wait_recv()
            g2(1 - i, q).start()

    pl.when(high)(lambda: pass_sideways(0))
    pl.when(high & (loop >= 4))(lambda: pass_sideways(1))
    id_f.wait_recv()

    @pl.when(high | (core == 0))
    def _():
        id_o.start()

    @pl.when(high)
    def _():
        for i in range(2):
            for q in range(PIECES):
                g2(i, q).wait_recv()

            @pl.when(core == 1)
            def _():
                for h in range(2):
                    go(i, h).start()

    for i, q in pieces(PIECES):
        gw(i, q).wait_recv()
    for i in range(2):
        for q in range(PIECES):
            gf(i, q).wait_recv()

        @pl.when(core == 0)
        def _():
            go(1, i).start()

    id_h.wait_recv()
    for s in range(4):
        keys[s * R:(s + 1) * R, :] = jnp.transpose(jnp.broadcast_to(idi[s], (128, R)))
    for i, q in pieces(PIECES):
        gh(i, q).wait_recv()

    scale_value, bias_value = scale[0], bias[0]

    def pair(b):
        return pl.ds(b * 2 * R if isinstance(b, int) else pl.multiple_of(b * 2 * R, 2 * R), 2 * R)

    def weigh(b):
        for a in range(4 * R // ROWS_AT_ONCE):
            rows = slice(a * ROWS_AT_ONCE, (a + 1) * ROWS_AT_ONCE)
            dots = lax.dot_general(
                img[rows, :], txt[pair(b), :], (((1,), (1,)), ((), ())), preferred_element_type=F32)
            logits = scale_value * dots + bias_value
            mine = keys[rows, :]
            same = jnp.concatenate([mine == idt[2 * b], mine == idt[2 * b + 1]], axis=1)
            share = jax.nn.sigmoid(jnp.where(same, -logits, logits))
            weights = jnp.where(same, -share, share)
            w[rows, pair(b)] = weights.astype(BF16)
            wt[pair(b), rows] = jnp.transpose(weights).astype(BF16)

    def ro(i):
        return send(block(t_s, i), block(oc_r, i), ro_s.at[i], ro_r.at[i], other)

    def rd(i, q):
        return send(half(d_s, 0, i, q, PARTS), half(d_r, 0, i, q, PARTS), rd_s.at[i, q], rd_r.at[i, q], x_near[1 - i])

    def rc(i, q):
        return send(half(t_s, 2 + i, 1 - i, q, PARTS), half(c_r, 0, 1 - i, q, PARTS), rc_s.at[i, q], rc_r.at[i, q], x_near[i])

    def rz(i, q):
        return send(half(t_s, 2 + i, i, q, PARTS), half(z_r, 0, i, q, PARTS), rz_s.at[i, q], rz_r.at[i, q], z_down)

    def rz_on(i, q):
        return send(half(c_r, 0, i, q, PARTS), half(z_r, 0, i, q, PARTS), rz_s.at[i, q], rz_r.at[i, q], z_down)

    def rx(i, q):
        return send(half(x_s, 0, i, q, PARTS), half(x_r, 0, i, q, PARTS), rx_s.at[i, q], rx_r.at[i, q], x_near[i])

    def rh(i, q):
        return send(half(h_s, 0, i, q, PARTS), half(h_r, 0, i, q, PARTS), rh_s.at[i, q], rh_r.at[i, q], y_near[i])

    def rn(i, q):
        return send(half(y_s, i, 1 - i, q, PARTS), half(y_r, i, 1 - i, q, PARTS), rn_s.at[i, q], rn_r.at[i, q], y_near[i])

    def ra(i, q):
        return send(half(y_s, i, i, q, PARTS), half(y_r, i, i, q, PARTS), ra_s.at[i, q], ra_r.at[i, q], y_near[i])

    def text_part(b):
        return jnp.dot(wt[pair(b), :], img[...], preferred_element_type=F32)

    def image_part(a):
        return jnp.dot(w[a * 2 * R:(a + 1) * 2 * R, :], txt[0:6 * R, :], preferred_element_type=F32)

    def send_far():
        d_s[...] = gt[R:2 * R, :].astype(BF16)
        for i, q in pieces(PARTS):
            rd(i, q).start()

    def send_cross():
        for i, q in pieces(PARTS):
            rc(i, q).start()

        @pl.when(low)
        def _():
            for i, q in pieces(PARTS):
                rz(i, q).start()

    weigh(0)
    gt[0:2 * R, :] = text_part(0)
    pl.when(core == 1)(send_far)
    pl.when(high & (loop < 4))(lambda: pass_sideways(1))

    def from_below():
        id_z.wait_recv()

        @pl.when(core == 1)
        def _():
            id_o.start()

        for i in range(2):
            for q in range(PIECES):
                gz(i, q).wait_recv()

            @pl.when(core == 1)
            def _():
                go(i, i).start()

        for i in range(2):
            for q in range(PIECES):
                g2(i, q).wait_recv()

            @pl.when(core == 1)
            def _():
                go(i, 1 - i).start()

    def from_other():
        id_o.wait_recv()
        for i in range(2):
            for h in range(2):
                go(i, h).wait_recv()

    def image_far():
        part = image_part(1)
        h_s[...] = part[R:2 * R].astype(BF16)
        gi[2 * R:3 * R, :] = part[0:R]
        y_s[H:R, :] = part[H:R].astype(BF16)
        for i, q in pieces(PARTS):
            rh(i, q).start()
        for q in range(PARTS):
            rn(0, q).start()

    def image_near():
        part = image_part(0)
        gi[0:2 * R, :] = part
        y_s[R:R + H, :] = part[R:R + H].astype(BF16)
        for q in range(PARTS):
            rn(1, q).start()

    pl.when(low)(from_below)
    pl.when(core == 1)(from_other)
    weigh(2 - core)
    t_s[pair(1 - core), :] = text_part(2 - core).astype(BF16)

    @pl.when(core == 1)
    def _():
        for i in range(2):
            ro(i).start()

    pl.when(core == 0)(send_cross)

    pl.when(core == 0)(from_other)
    weigh(1 + core)

    @pl.when(core == 0)
    def _():
        for i in range(2):
            ro(i).wait_recv()
        gt[0:2 * R, :] = gt[0:2 * R, :] + oc_r[...].astype(F32)
        send_far()


    gt[2 * R:4 * R, :] = text_part(1 + core)

    @pl.when(core == 0)
    def _():
        t_s[0:2 * R, :] = gt[2 * R:4 * R, :].astype(BF16)
        for i in range(2):
            ro(i).start()

    image_far()
    @pl.when(core == 1)
    def _():
        for i in range(2):
            ro(i).wait_recv()
        t_s[2 * R:4 * R, :] = (gt[2 * R:4 * R, :] + oc_r[...].astype(F32)).astype(BF16)
        send_cross()

    image_near()


    def piece(h, q):
        return slice(h * H + q * (H // PARTS), h * H + (q + 1) * (H // PARTS))

    def shifted(at, slot):
        return slice(slot * R + at.start, slot * R + at.stop)

    for i, q in pieces(PARTS):
        rh(i, q).wait_recv()
        at = piece(i, q)
        y_s[shifted(at, i), :] = (gi[shifted(at, 2 - i), :] + h_r[at, :].astype(F32)).astype(BF16)
        ra(i, q).start()

    @pl.when(high)
    def _():
        for i, q in pieces(PARTS):
            rc(i, q).wait_recv()
            rz_on(1 - i, q).start()

    def send_near(i, q, first):
        at = piece(i, q)
        x_s[at, :] = (first.astype(F32) + d_r[at, :].astype(F32)).astype(BF16)
        rx(i, q).start()

    for i, q in pieces(PARTS):
        rd(i, q).wait_recv()

        @pl.when(low)
        def _():
            rz(i, q).wait_recv()
            send_near(i, q, z_r[piece(i, q), :])

        @pl.when(high)
        def _():
            send_near(i, q, t_s[shifted(piece(i, q), 2 + i), :])

    def backward(rows, total, out):
        values = rows[...].astype(F32)
        factor = 1.0 / jnp.sqrt(jnp.sum(values * values, axis=-1, keepdims=True) + epsilon)
        unit = values * factor
        grad = total
        along = jnp.sum(unit * grad, axis=-1, keepdims=True)
        out[...] = factor * (grad - unit * along)

    for i, q in pieces(PARTS):
        rn(i, q).wait_recv()
        ra(i, q).wait_recv()
    backward(raw_i, gi[0:R, :] + (y_r[0:R, :].astype(F32) + y_r[R:2 * R, :].astype(F32)), image_out)

    @pl.when(high)
    def _():
        for i, q in pieces(PARTS):
            rz(i, q).wait_recv()
        gt[R:2 * R, :] = gt[0:R, :] + z_r[...].astype(F32)

    @pl.when(low)
    def _():
        for i, q in pieces(PARTS):
            rc(i, q).wait_recv()
        gt[R:2 * R, :] = gt[0:R, :] + c_r[...].astype(F32)

    for i, q in pieces(PARTS):
        rx(i, q).wait_recv()
    backward(raw_t, gt[R:2 * R, :] + x_r[...].astype(F32), text_out)

    for copy in (gx, g2, gf, gz, gy, gw, gh):
        for i, q in pieces(PIECES):
            copy(i, q).wait_send()
    for copy in (rd, rc, rz, rx, rh, rn, ra):
        for i, q in pieces(PARTS):
            copy(i, q).wait_send()
    for i in range(2):
        for h in range(2):
            go(i, h).wait_send()
        ro(i).wait_send()
    for copy in id_x + id_y + [id_f, id_o, id_h]:
        copy.wait_send()

    @pl.when(low)
    def _():
        id_z.wait_send()


def shards(n_loop, images, texts, image_ids, text_ids, logit_scale, logit_bias):
    R, D = images.shape
    dma = pltpu.SemaphoreType.DMA
    vmem = pl.BlockSpec(memory_space=pltpu.VMEM)
    smem = pl.BlockSpec(memory_space=pltpu.SMEM)
    anywhere = pl.BlockSpec(memory_space=pltpu.HBM)

    def rows(count, dtype=BF16):
        return pltpu.VMEM((count * R, D), dtype)

    image_rows, text_rows = pl.pallas_call(
        functools.partial(kernel, n_loop),
        out_shape=(pltpu.VMEM((R, D), F32), pltpu.VMEM((R, D), F32)),
        in_specs=[anywhere, anywhere, anywhere, anywhere, smem, smem],
        out_specs=(vmem, vmem),
        scratch_shapes=[
            rows(1), rows(1), rows(4), rows(8),
            pltpu.VMEM((4, 1, R), jnp.int32), pltpu.VMEM((8, 1, R), jnp.int32), pltpu.VMEM((4 * R, 128), jnp.int32),
            pltpu.VMEM((4 * R, 6 * R), BF16), pltpu.VMEM((6 * R, 4 * R), BF16), rows(4, F32), rows(3, F32),
            rows(4), rows(2), rows(1), rows(1), rows(1), rows(1), rows(1), rows(1), rows(1), rows(1),
            rows(2), rows(2), dma((4,)),
        ] + [dma((2, PIECES))] * 8 + [dma((2, 2))] * 2 + [dma((2, PIECES))] * 6 + [dma((8,))] * 2
        + [dma((2,))] * 2 + [dma((2, PARTS))] * 14,
        compiler_params=pltpu.CompilerParams(
            collective_id=0, has_side_effects=True, vmem_limit_bytes=24 * 1024 * 1024),
        cost_estimate=pl.CostEstimate(
            flops=6 * 4 * R * 6 * R * D, bytes_accessed=12 * R * D, transcendentals=24 * R * R),
    )(*[pltpu.with_memory_space_constraint(x, pltpu.HBM)
        for x in (images, texts, image_ids.reshape(1, R), text_ids.reshape(1, R))], logit_scale, logit_bias)
    return image_rows * logit_scale[0], text_rows * logit_scale[0]


def solution(mesh):
    rows = P(("loop", "group"), None)
    ids = P(("loop", "group"))
    return jax.shard_map(
        functools.partial(shards, mesh.shape["loop"]), mesh=mesh,
        in_specs=(rows, rows, ids, ids, P(), P()), out_specs=(rows, rows), check_vma=False)
```

time: 48.6 us -> 43.9 us (0.903)
  Pallas kernels: 44.2 us -> 40.7 us
  other arithmetic: 2.33 us -> 1.09 us
    pallas_call x1, Pallas kernels: 44.2 us -> 40.7 us  [shards(): pl.pallas_call(functools.partial(kernel, n_loop), out_shape=(pltpu.VMEM((...]
    mul x1, other arithmetic: 2.33 us -> 1.09 us  [shards(): return (image_rows * logit_scale[0], text_rows * logit_scale[0])]
where the time goes in v4:
time: 43.9 us; the launch traced here: 43.7 us
  Pallas kernels  40.7 us (93%)
  between operations  1.93 us (4%)
  other arithmetic  1.09 us (2%)
    pallas_call x1, Pallas kernels, shards(): pl.pallas_call(functools.partial(kernel, n_loop), out_shape=(pltpu.VMEM((...  40.7 us
    mul x1, other arithmetic, shards(): return (image_rows * logit_scale[0], text_rows * logit_scale[0])  1.09 us

profile of v4, /device:TPU:1, one launch (start us, length us, event | category | flops | bytes accessed | tf_op | source)
XLA Modules:
  0.0 43.7 jit_solution(13706968613017382484)
XLA Ops:
  1.9 40.7 %shard_map.77 = (f32[128,1152]{1,0:T(8,128)S(1)}, f32[128,1152]{1,0:T(8,128)S(1)}) custom-call(bf16[128,1152]{1,0:T(8,128)(2,1)} %images.1, bf16[128,1152]{1,0:T(8,128)(2,1)} %texts.1, s32[1,128]{1,0:T(1,128)} %bitcast.4, s32[1,128]{1,0:T(1,128)} %bitcast.5, f32[1]{0:T(128)} %copy.8.scale, f32[1]{0:T(128)S(6)} %copy.9.bias), custom_call_target="tpu_custom_call" | custom-call | flops 2717908992 | bytes 1769472 | tf_op jit(solution)/shard_map/pallas_call | solution.py:450
  42.7 1.1 %broadcast_multiply_fusion = (f32[128,1152]{1,0:T(8,128)}, f32[128,1152]{1,0:T(8,128)}) fusion(f32[128,1152]{1,0:T(8,128)S(1)} %get-tuple-element.5, f32[]{:T(128)} %bitcast.3, f32[128,1152]{1,0:T(8,128)S(1)} %get-tuple-element.4), kind=kLoop, calls=%fused_computation | loop fusion | flops 294912 | bytes 2359300 | tf_op jit(solution)/shard_map/mul | solution.py:469

commit v5 on v4

--- a/solution.py
+++ b/solution.py
@@ -262,11 +262,6 @@
             for i, q in pieces(PARTS):
                 rz(i, q).start()
 
-    weigh(0)
-    gt[0:2 * R, :] = text_part(0)
-    pl.when(core == 1)(send_far)
-    pl.when(high & (loop < 4))(lambda: pass_sideways(1))
-
     def from_below():
         id_z.wait_recv()
 
@@ -313,6 +308,10 @@
         for q in range(PARTS):
             rn(1, q).start()
 
+    weigh(0)
+    gt[0:2 * R, :] = text_part(0)
+    pl.when(core == 1)(send_far)
+    pl.when(high & (loop < 4))(lambda: pass_sideways(1))
     pl.when(low)(from_below)
     pl.when(core == 1)(from_other)
     weigh(2 - core)
@@ -324,9 +323,9 @@
             ro(i).start()
 
     pl.when(core == 0)(send_cross)
-
     pl.when(core == 0)(from_other)
     weigh(1 + core)
+    image_far()
 
     @pl.when(core == 0)
     def _():
@@ -335,7 +334,6 @@
         gt[0:2 * R, :] = gt[0:2 * R, :] + oc_r[...].astype(F32)
         send_far()
 
-
     gt[2 * R:4 * R, :] = text_part(1 + core)
 
     @pl.when(core == 0)
@@ -344,7 +342,7 @@
         for i in range(2):
             ro(i).start()
 
-    image_far()
+
     @pl.when(core == 1)
     def _():
         for i in range(2):
@@ -354,24 +352,23 @@
 
     image_near()
 
-
     def piece(h, q):
         return slice(h * H + q * (H // PARTS), h * H + (q + 1) * (H // PARTS))
 
     def shifted(at, slot):
         return slice(slot * R + at.start, slot * R + at.stop)
+
+    @pl.when(high)
+    def _():
+        for i, q in pieces(PARTS):
+            rc(i, q).wait_recv()
+            rz_on(1 - i, q).start()
 
     for i, q in pieces(PARTS):
         rh(i, q).wait_recv()
         at = piece(i, q)
         y_s[shifted(at, i), :] = (gi[shifted(at, 2 - i), :] + h_r[at, :].astype(F32)).astype(BF16)
         ra(i, q).start()
-
-    @pl.when(high)
-    def _():
-        for i, q in pieces(PARTS):
-            rc(i, q).wait_recv()
-            rz_on(1 - i, q).start()
 
     def send_near(i, q, first):
         at = piece(i, q)

time: 43.9 us -> 44 us (level)
  no operation moved by 1% of the time
where the time goes in v5:
time: 44 us; the launch traced here: 43.9 us
  Pallas kernels  40.9 us (93%)
  between operations  1.93 us (4%)
  other arithmetic  1.09 us (2%)
    pallas_call x1, Pallas kernels, shards(): pl.pallas_call(functools.partial(kernel, n_loop), out_shape=(pltpu.VMEM((...  40.9 us
    mul x1, other arithmetic, shards(): return (image_rows * logit_scale[0], text_rows * logit_scale[0])  1.09 us

profile of v5, /device:TPU:1, one launch (start us, length us, event | category | flops | bytes accessed | tf_op | source)
XLA Modules:
  0.0 43.9 jit_solution(4557224756934144719)
XLA Ops:
  1.9 40.9 %shard_map.77 = (f32[128,1152]{1,0:T(8,128)S(1)}, f32[128,1152]{1,0:T(8,128)S(1)}) custom-call(bf16[128,1152]{1,0:T(8,128)(2,1)} %images.1, bf16[128,1152]{1,0:T(8,128)(2,1)} %texts.1, s32[1,128]{1,0:T(1,128)} %bitcast.4, s32[1,128]{1,0:T(1,128)} %bitcast.5, f32[1]{0:T(128)} %copy.8.scale, f32[1]{0:T(128)S(6)} %copy.9.bias), custom_call_target="tpu_custom_call" | custom-call | flops 2717908992 | bytes 1769472 | tf_op jit(solution)/shard_map/pallas_call | solution.py:447
  42.8 1.1 %broadcast_multiply_fusion = (f32[128,1152]{1,0:T(8,128)}, f32[128,1152]{1,0:T(8,128)}) fusion(f32[128,1152]{1,0:T(8,128)S(1)} %get-tuple-element.5, f32[]{:T(128)} %bitcast.3, f32[128,1152]{1,0:T(8,128)S(1)} %get-tuple-element.4), kind=kLoop, calls=%fused_computation | loop fusion | flops 294912 | bytes 2359300 | tf_op jit(solution)/shard_map/mul | solution.py:466

commit v6 on v5

--- a/solution.py
+++ b/solution.py
@@ -44,8 +44,13 @@
     for copy in loads:
         copy.start()
     barrier = pltpu.get_barrier_semaphore()
-    for device in (*x_near, *y_near, z_down, other):
-        pl.semaphore_signal(barrier, inc=1, device_id=device, device_id_type=MESH)
+
+    def signal(*others):
+        for device in others:
+            pl.semaphore_signal(barrier, inc=1, device_id=device, device_id_type=MESH)
+
+    signal(*x_near, *y_near, z_down)
+    pl.when(core == 1)(lambda: signal(other))
 
     def normalize(rows, block):
         values = rows[...].astype(F32)
@@ -107,7 +112,7 @@
     normalize(raw_t, txt)
     loads[2].wait()
     loads[3].wait()
-    pl.semaphore_wait(barrier, 6)
+    pl.semaphore_wait(barrier, 6 - core)
     for copy in id_x + id_y:
         copy.start()
     for i, q in pieces(PIECES):
@@ -135,6 +140,40 @@
         for h in range(2):
             go(0, h).start()
 
+    def x_step(i, q):
+        gx(i, q).wait_recv()
+        gf(i, q).start()
+
+        @pl.when(low)
+        def _():
+            gz(i, q).start()
+
+    def y_step(i, q):
+        gy(i, q).wait_recv()
+        gh(i, q).start()
+
+    def pass_on(q):
+        @pl.when(x_hi == 0)
+        def _():
+            x_step(1, q)
+            x_step(0, q)
+
+        @pl.when(x_hi == 1)
+        def _():
+            x_step(0, q)
+            x_step(1, q)
+
+        @pl.when(y < 2)
+        def _():
+            y_step(1, q)
+            y_step(0, q)
+
+        @pl.when(y >= 2)
+        def _():
+            y_step(0, q)
+            y_step(1, q)
+
+    pass_on(0)
     for copy in id_x + id_y:
         copy.wait_recv()
     id_f.start()
@@ -144,18 +183,8 @@
     def _():
         id_z.start()
 
-    for q in range(PIECES):
-        for i in range(2):
-            gx(i, q).wait_recv()
-            gf(i, q).start()
-
-            @pl.when(low)
-            def _():
-                gz(i, q).start()
-
-        for i in range(2):
-            gy(i, q).wait_recv()
-            gh(i, q).start()
+    for q in range(1, PIECES):
+        pass_on(q)
 
     def pass_sideways(q):
         for i in range(2):
@@ -165,6 +194,10 @@
     pl.when(high)(lambda: pass_sideways(0))
     pl.when(high & (loop >= 4))(lambda: pass_sideways(1))
     id_f.wait_recv()
+
+    @pl.when(high & (core == 1))
+    def _():
+        go(0, 0).wait_recv()
 
     @pl.when(high | (core == 0))
     def _():
@@ -248,18 +281,18 @@
     def image_part(a):
         return jnp.dot(w[a * 2 * R:(a + 1) * 2 * R, :], txt[0:6 * R, :], preferred_element_type=F32)
 
-    def send_far():
-        d_s[...] = gt[R:2 * R, :].astype(BF16)
+    def send_far(more=0.0):
+        d_s[...] = (gt[R:2 * R, :] + more).astype(BF16)
         for i, q in pieces(PARTS):
             rd(i, q).start()
 
-    def send_cross():
-        for i, q in pieces(PARTS):
+    def send_cross(i):
+        for q in range(PARTS):
             rc(i, q).start()
 
         @pl.when(low)
         def _():
-            for i, q in pieces(PARTS):
+            for q in range(PARTS):
                 rz(i, q).start()
 
     def from_below():
@@ -267,6 +300,7 @@
 
         @pl.when(core == 1)
         def _():
+            go(0, 0).wait_recv()
             id_o.start()
 
         for i in range(2):
@@ -287,9 +321,9 @@
 
     def from_other():
         id_o.wait_recv()
-        for i in range(2):
-            for h in range(2):
-                go(i, h).wait_recv()
+        pl.when(core == 0)(go(0, 0).wait_recv)
+        for i, h in ((0, 1), (1, 0), (1, 1)):
+            go(i, h).wait_recv()
 
     def image_far():
         part = image_part(1)
@@ -319,36 +353,39 @@
 
     @pl.when(core == 1)
     def _():
-        for i in range(2):
+        for i in (1, 0):
             ro(i).start()
 
-    pl.when(core == 0)(send_cross)
+    @pl.when(core == 0)
+    def _():
+        for i in range(2):
+            send_cross(i)
+
     pl.when(core == 0)(from_other)
     weigh(1 + core)
     image_far()
 
     @pl.when(core == 0)
     def _():
+        ro(1).wait_recv()
+        send_far(oc_r[R:2 * R, :].astype(F32))
+
+    gt[2 * R:4 * R, :] = text_part(1 + core)
+
+    @pl.when(core == 0)
+    def _():
+        t_s[0:2 * R, :] = gt[2 * R:4 * R, :].astype(BF16)
+        for i in range(2):
+            ro(i).start()
+
+
+    @pl.when(core == 1)
+    def _():
         for i in range(2):
             ro(i).wait_recv()
-        gt[0:2 * R, :] = gt[0:2 * R, :] + oc_r[...].astype(F32)
-        send_far()
-
-    gt[2 * R:4 * R, :] = text_part(1 + core)
-
-    @pl.when(core == 0)
-    def _():
-        t_s[0:2 * R, :] = gt[2 * R:4 * R, :].astype(BF16)
-        for i in range(2):
-            ro(i).start()
-
-
-    @pl.when(core == 1)
-    def _():
-        for i in range(2):
-            ro(i).wait_recv()
-        t_s[2 * R:4 * R, :] = (gt[2 * R:4 * R, :] + oc_r[...].astype(F32)).astype(BF16)
-        send_cross()
+            at = slice((2 + i) * R, (3 + i) * R)
+            t_s[at, :] = (gt[at, :] + oc_r[i * R:(i + 1) * R, :].astype(F32)).astype(BF16)
+            send_cross(i)
 
     image_near()
 
@@ -399,6 +436,11 @@
         rn(i, q).wait_recv()
         ra(i, q).wait_recv()
     backward(raw_i, gi[0:R, :] + (y_r[0:R, :].astype(F32) + y_r[R:2 * R, :].astype(F32)), image_out)
+
+    @pl.when(core == 0)
+    def _():
+        ro(0).wait_recv()
+        gt[0:R, :] = gt[0:R, :] + oc_r[0:R, :].astype(F32)
 
     @pl.when(high)
     def _():

time: 44 us -> 43.8 us (level)
  no operation moved by 1% of the time
where the time goes in v6:
time: 43.8 us; the launch traced here: 43.7 us
  Pallas kernels  40.7 us (93%)
  between operations  1.93 us (4%)
  other arithmetic  1.09 us (2%)
    pallas_call x1, Pallas kernels, shards(): pl.pallas_call(functools.partial(kernel, n_loop), out_shape=(pltpu.VMEM((...  40.7 us
    mul x1, other arithmetic, shards(): return (image_rows * logit_scale[0], text_rows * logit_scale[0])  1.09 us

profile of v6, /device:TPU:1, one launch (start us, length us, event | category | flops | bytes accessed | tf_op | source)
XLA Modules:
  0.0 43.7 jit_solution(9803306279334935976)
XLA Ops:
  1.9 40.7 %shard_map.77 = (f32[128,1152]{1,0:T(8,128)S(1)}, f32[128,1152]{1,0:T(8,128)S(1)}) custom-call(bf16[128,1152]{1,0:T(8,128)(2,1)} %images.1, bf16[128,1152]{1,0:T(8,128)(2,1)} %texts.1, s32[1,128]{1,0:T(1,128)} %bitcast.4, s32[1,128]{1,0:T(1,128)} %bitcast.5, f32[1]{0:T(128)} %copy.8.scale, f32[1]{0:T(128)S(6)} %copy.9.bias), custom_call_target="tpu_custom_call" | custom-call | flops 2717908992 | bytes 1769472 | tf_op jit(solution)/shard_map/pallas_call | solution.py:489
  42.6 1.1 %broadcast_multiply_fusion = (f32[128,1152]{1,0:T(8,128)}, f32[128,1152]{1,0:T(8,128)}) fusion(f32[128,1152]{1,0:T(8,128)S(1)} %get-tuple-element.5, f32[]{:T(128)} %bitcast.3, f32[128,1152]{1,0:T(8,128)S(1)} %get-tuple-element.4), kind=kLoop, calls=%fused_computation | loop fusion | flops 294912 | bytes 2359300 | tf_op jit(solution)/shard_map/mul | solution.py:508
